TPU v7x, 32 devices: a whole 2x2x4 slice. The times are simulated.
32 devices in a mesh: dp: 4 (over x, core), fsdp: 8 (over z, y).
Axes of the slice: x: 2, y: 2, z: 4, core: 2. Of those that a mesh axis runs over, the one named last changes fastest.
Arguments:
- tokens: bfloat16 [16384, 1024], P(('dp', 'fsdp')), may hold values from -6 to 6
- segments: int32 [32, 512], P(('dp', 'fsdp')), may hold values from 0 to 3, never falling along the last dimension, each value on 1 to 256 neighbouring positions
- mixer_gain: bfloat16 [1024], P('fsdp'), may hold values from 0.099609375 to 1.8984375
- in_weight: bfloat16 [1024, 3072], P('fsdp', 'dp'), may hold values from -0.1875 to 0.1875
- conv_kernel: bfloat16 [1024, 3], P('fsdp'), may hold values from -3.5 to 3.5
- out_weight: bfloat16 [1024, 1024], P('fsdp', 'dp'), may hold values from -0.1875 to 0.1875
- ffn_gain: bfloat16 [1024], P('fsdp'), may hold values from 0.099609375 to 1.8984375
- gate_weight: bfloat16 [1024, 4608], P('fsdp', 'dp'), may hold values from -0.1875 to 0.1875
- up_weight: bfloat16 [1024, 4608], P('fsdp', 'dp'), may hold values from -0.1875 to 0.1875
- down_weight: bfloat16 [1024, 4608], P('fsdp', 'dp'), may hold values from -0.09375 to 0.09375
- cotangent: bfloat16 [16384, 1024], P(('dp', 'fsdp')), may hold values from -6 to 6
Outputs:
- output: bfloat16 [16384, 1024], P(('dp', 'fsdp'))
- input_grad: float32 [16384, 1024], P(('dp', 'fsdp'))
- mixer_gain_grad: float32 [1024], P('fsdp')
- in_weight_grad: float32 [1024, 3072], P('fsdp', 'dp')
- conv_kernel_grad: float32 [1024, 3], P('fsdp')
- out_weight_grad: float32 [1024, 1024], P('fsdp', 'dp')
- ffn_gain_grad: float32 [1024], P('fsdp')
- gate_weight_grad: float32 [1024, 4608], P('fsdp', 'dp')
- up_weight_grad: float32 [1024, 4608], P('fsdp', 'dp')
- down_weight_grad: float32 [1024, 4608], P('fsdp', 'dp')
Inputs may be any that keep to these rules, and one draw needn't show every extreme that they name: `segments`: in each sequence the document numbers never fall, start at 0, and each document has 1 to 256 tokens, one exactly 256.
All inputs are finite; a program needn't handle non-finite values.
Results may differ from a plain program's by a relative error of at most 0.0091.
Values may be sent and summed in bfloat16 or wider, within the bound.
No kernel may reach another device: no remote copies, remote signals or barrier semaphores. Data moves between devices by JAX's collectives and lax.ppermute only.
A program may use at most 256 MiB of HBM per device.

v0:
```python
import functools

import jax
import jax.numpy as jnp
from jax import lax
from jax.experimental import pallas as pl
from jax.experimental.pallas import tpu as pltpu
from jax.sharding import PartitionSpec as P

EPSILON = 1e-05
LINK = jnp.bfloat16
F32 = jnp.float32
PAD = 128
MIB = 1 << 20


def dot_plain(left, right):
    return jnp.dot(left, right, preferred_element_type=F32)


def dot_rows(left, right):
    return lax.dot_general(left, right, (((0,), (0,)), ((), ())), preferred_element_type=F32)


def dot_last(left, right):
    return lax.dot_general(left, right, (((1,), (1,)), ((), ())), preferred_element_type=F32)


def after(v, *others):
    return lax.optimization_barrier((v, *others))[0]


def shape(dims, dtype):
    return jax.ShapeDtypeStruct(dims, dtype)


SCALARS = pl.BlockSpec(memory_space=pltpu.SMEM)
WHOLE = pl.BlockSpec(memory_space=pltpu.VMEM)
APART = pl.BlockSpec(memory_space=pl.ANY)


def call(kernel, scalars, args, outs, flops=0, limit=40, scratch=(), apart=0, deps=()):
    moved = sum(a.size * a.dtype.itemsize for a in args) + sum(
        o.size * jnp.dtype(o.dtype).itemsize for o in outs
    )
    first, last = 1 + len(args), 1 + len(args) + len(deps)

    def run(*refs):
        kernel(*refs[:first], *refs[last:])

    return pl.pallas_call(
        run,
        out_shape=outs,
        in_specs=[SCALARS] + [WHOLE] * len(args) + [APART] * len(deps),
        out_specs=[WHOLE] * (len(outs) - apart) + [APART] * apart,
        scratch_shapes=list(scratch),
        compiler_params=pltpu.CompilerParams(vmem_limit_bytes=limit * MIB),
        cost_estimate=pl.CostEstimate(flops=flops, bytes_accessed=moved, transcendentals=0),
    )(scalars, *args, *deps)


def pack_kernel(where_ref, in_ref, out_ref, one_ref, two_ref, taps_ref, packed_ref):
    rows = in_ref.shape[0]
    in_half, out_half = in_ref.shape[1] // 2, out_ref.shape[1] // 2
    cut = in_half + out_half
    packed_ref[:, :in_half] = in_ref[:, :in_half]
    packed_ref[:, in_half:cut] = out_ref[:, :out_half]
    packed_ref[:, cut : cut + in_half] = in_ref[:, in_half:]
    packed_ref[:, cut + in_half : 2 * cut] = out_ref[:, out_half:]
    eye = lax.broadcasted_iota(jnp.int32, (rows, rows), 0) == lax.broadcasted_iota(
        jnp.int32, (rows, rows), 1
    )
    lane = lax.broadcasted_iota(jnp.int32, (rows, PAD), 1)
    small = jnp.zeros((rows, PAD), F32)
    for k, ref in enumerate((one_ref, two_ref)):
        column = jnp.sum(jnp.where(eye, ref[...].astype(F32), 0.0), axis=1, keepdims=True)
        small = jnp.where(lane == k, column, small)
    for k in range(3):
        small = jnp.where(lane == 2 + k, taps_ref[:, k : k + 1].astype(F32), small)
    packed_ref[:, 2 * cut :] = small.astype(LINK)


def merge_kernel(where_ref, *refs):
    pieces, (first_ref, second_ref, small_ref) = refs[:-3], refs[-3:]
    rows = pieces[0].shape[0]
    high = where_ref[2]
    cut = first_ref.shape[1]
    for s, piece in enumerate(pieces):
        spot = high - s
        spot = jnp.where(spot < 0, spot + len(pieces), spot)
        at = pl.ds(pl.multiple_of(spot * rows, rows), rows)
        first_ref[at, :] = piece[:, :cut]
        second_ref[at, :] = piece[:, cut : 2 * cut]
        small_ref[at, :] = piece[:, 2 * cut :]


def natural(low, near, away, put, rows, blocks):
    def one(h, carry):
        at = pl.ds(pl.multiple_of(h * rows, rows), rows)
        put(pl.ds(pl.multiple_of((2 * h + low) * rows, rows), rows), at, near)
        put(pl.ds(pl.multiple_of((2 * h + 1 - low) * rows, rows), rows), at, away)
        return carry

    lax.fori_loop(0, blocks, one, 0)


def mixer_weights_kernel(rows, where_ref, *refs):
    pieces, (in_ref, out_ref) = refs[:16], refs[16:18]
    low, place = where_ref[0], where_ref[1]
    in_half, out_half = in_ref.shape[1] // 8, out_ref.shape[1] // 8
    for k in range(8):
        half, r = k // 4, k % 4
        block = lax.bitwise_xor(place, r)
        in_at = pl.ds(pl.multiple_of((2 * block + half) * in_half, PAD), in_half)
        out_at = pl.ds(pl.multiple_of((2 * block + half) * out_half, PAD), out_half)

        def put(to, at, ref):
            in_ref[to, in_at] = ref[at, :in_half]
            out_ref[to, out_at] = ref[at, in_half:]

        natural(low, pieces[2 * k], pieces[2 * k + 1], put, rows, pieces[0].shape[0] // rows)


def back_rows(v, steps):
    return pltpu.roll(v, steps, 0)


def ahead_rows(v, steps):
    return pltpu.roll(v, v.shape[0] - steps, 0)


def small_rows(rows, low, near_ref, away_ref, small_ref):
    def put(to, at, ref):
        small_ref[to, :] = ref[at, :].astype(F32)

    natural(low, near_ref, away_ref, put, rows, near_ref.shape[0] // rows)
    return small_ref[...].T[:8]


def mixer_kernel(
    rows,
    where_ref,
    tokens_ref,
    same_ref,
    near_ref,
    away_ref,
    *refs,
):
    pieces = refs[:16]
    normed_ref, parts_ref, scaled_ref, hidden_ref, next_ref, gains_ref = refs[16:22]
    small_ref, in_ref, outw_ref, in_sem, outw_sem = refs[24:]
    mixer_weights_kernel(rows, where_ref, *pieces, in_ref, outw_ref)
    in_copy = pltpu.make_async_copy(in_ref, refs[22], in_sem)
    outw_copy = pltpu.make_async_copy(outw_ref, refs[23], outw_sem)
    in_copy.start()
    outw_copy.start()
    width = tokens_ref.shape[1]
    step = 256
    gains_ref[...] = small_rows(rows, where_ref[0], near_ref, away_ref, small_ref)
    inputs = tokens_ref[...].astype(F32)
    inverse = lax.rsqrt(jnp.mean(inputs * inputs, axis=1, keepdims=True) + EPSILON)
    normed_ref[...] = (inputs * inverse * gains_ref[0:1, :]).astype(LINK)

    def chunk(q, carry):
        at = pl.ds(q * step, step)

        def part(k):
            w = in_ref[:, pl.ds(k * width + q * step, step)]
            v = dot_plain(normed_ref[...], w)
            parts_ref[k, :, at] = v
            return v

        b_part = part(0)
        x_part = part(2)
        gated = b_part * x_part
        mixed = (
            gains_ref[2:3, at] * gated
            + gains_ref[3:4, at] * (back_rows(gated, 1) * same_ref[:, 0:1])
            + gains_ref[4:5, at] * (back_rows(gated, 2) * same_ref[:, 1:2])
        )
        scaled_ref[:, at] = (part(1) * mixed).astype(LINK)
        return carry

    for q in range(width // step):
        chunk(q, 0)

    def final(q, total):
        at = pl.ds(q * step, step)
        v = tokens_ref[:, at].astype(F32) + dot_last(scaled_ref[...], outw_ref[at, :])
        hidden_ref[:, at] = v
        return total + jnp.sum(v * v, axis=1, keepdims=True)

    total = jnp.zeros((tokens_ref.shape[0], 1), F32)
    for q in range(width // step):
        total = final(q, total)
    inverse_two = lax.rsqrt(total / width + EPSILON)
    next_ref[...] = (hidden_ref[...] * inverse_two * gains_ref[1:2, :]).astype(LINK)
    in_copy.wait()
    outw_copy.wait()


def mixer_back_kernel(
    where_ref,
    own_ref,
    got_ref,
    far_one_ref,
    far_two_ref,
    hidden_ref,
    cot_ref,
    same_ref,
    gains_ref,
    parts_ref,
    outw_ref,
    hidden_grad_ref,
    branch_ref,
    proj_ref,
    sums_ref,
):
    width = hidden_ref.shape[1]
    step = 256
    hidden = hidden_ref[...]
    inverse = lax.rsqrt(jnp.mean(hidden * hidden, axis=1, keepdims=True) + EPSILON)
    far = jnp.concatenate([far_one_ref[...], far_two_ref[...]], axis=0)
    grad = own_ref[...].astype(F32) + got_ref[...].astype(F32) + far.astype(F32)
    sums_ref[0:1, :] = jnp.zeros((1, width), F32)
    sums_ref[1:2, :] = jnp.sum(grad * (hidden * inverse), axis=0, keepdims=True)
    weighted = grad * gains_ref[1:2, :]
    mean = jnp.mean(weighted * hidden, axis=1, keepdims=True)
    total = cot_ref[...].astype(F32) + inverse * (weighted - hidden * (inverse * inverse * mean))
    hidden_grad_ref[...] = total
    branch_ref[...] = total.astype(LINK)

    def chunk(q, carry):
        at = pl.ds(q * step, step)
        grad_scaled = dot_plain(branch_ref[...], outw_ref[:, at])
        b_part, c_part, x_part = (parts_ref[k, :, at] for k in range(3))
        same_one, same_two = same_ref[:, 0:1], same_ref[:, 1:2]
        gated = b_part * x_part
        back_one = back_rows(gated, 1) * same_one
        back_two = back_rows(gated, 2) * same_two
        taps = [gains_ref[2 + k : 3 + k, at] for k in range(3)]
        mixed = taps[0] * gated + taps[1] * back_one + taps[2] * back_two
        grad_mixed = grad_scaled * c_part
        sums_ref[2:3, at] = jnp.sum(grad_mixed * gated, axis=0, keepdims=True)
        sums_ref[3:4, at] = jnp.sum(grad_mixed * back_one, axis=0, keepdims=True)
        sums_ref[4:5, at] = jnp.sum(grad_mixed * back_two, axis=0, keepdims=True)
        grad_gated = (
            taps[0] * grad_mixed
            + taps[1] * ahead_rows(grad_mixed * same_one, 1)
            + taps[2] * ahead_rows(grad_mixed * same_two, 2)
        )
        for k, v in enumerate((grad_gated * x_part, grad_scaled * mixed, grad_gated * b_part)):
            proj_ref[:, pl.ds(k * width + q * step, step)] = v.astype(LINK)
        return carry

    for q in range(width // step):
        chunk(q, 0)
    sums_ref[5:8, :] = jnp.zeros((3, width), F32)


def mixer_grads_kernel(
    rows, order, where_ref, normed_ref, proj_ref, branch_ref, scaled_ref, *refs
):
    low, place = where_ref[0], where_ref[1]
    outs, (total_ref, held_ref, sems) = refs[:8], refs[8:]
    in_half = proj_ref.shape[1] // 8
    out_half = scaled_ref.shape[1] // 8
    for n in range(4):
        i, half = n // 2, n % 2
        block = 2 * lax.bitwise_xor(place, order[i]) + half
        in_at = pl.ds(pl.multiple_of(block * in_half, PAD), in_half)
        out_at = pl.ds(pl.multiple_of(block * out_half, PAD), out_half)
        total_ref[:, :in_half] = dot_rows(normed_ref[...], proj_ref[:, in_at])
        total_ref[:, in_half:] = dot_rows(branch_ref[...], scaled_ref[:, out_at])

        def copy(h, carry, n=n):
            to = pl.ds(pl.multiple_of(h * rows, rows), rows)
            for k, bit in enumerate((low, 1 - low)):
                at = pl.ds(pl.multiple_of((2 * h + bit) * rows, rows), rows)
                held_ref[2 * n + k, to, :] = total_ref[at, :].astype(LINK)
            return carry

        lax.fori_loop(0, held_ref.shape[1] // rows, copy, 0)
        for k in (2 * n, 2 * n + 1):
            pltpu.make_async_copy(held_ref.at[k], outs[k], sems.at[k]).start()
    for k in range(8):
        pltpu.make_async_copy(held_ref.at[k], outs[k], sems.at[k]).wait()


def final_kernel(where_ref, own_ref, *refs):
    gots, (in_ref, outw_ref, one_ref, two_ref, taps_ref) = refs[:-5], refs[-5:]
    in_half, out_half = in_ref.shape[1] // 2, outw_ref.shape[1] // 2
    cut = in_half + out_half

    def total(start, size):
        v = own_ref[:, start : start + size]
        for ref in gots:
            v = v + ref[:, start : start + size].astype(F32)
        return v

    for k in range(2):
        in_ref[:, k * in_half : (k + 1) * in_half] = total(k * cut, in_half)
        outw_ref[:, k * out_half : (k + 1) * out_half] = total(k * cut + in_half, out_half)
    small = total(2 * cut, PAD)
    turned = small.T
    one_ref[...] = turned[0:1]
    two_ref[...] = turned[1:2]
    taps_ref[...] = small[:, 2:5]


def join_kernel(where_ref, *refs):
    for k in range(2):
        a, b, c = (r[...].astype(F32) for r in refs[3 * k : 3 * k + 3])
        refs[6 + k][...] = (a + b + c).astype(LINK)


def add_kernel(where_ref, *refs):
    n = len(refs) // 3
    for a, b, c in zip(refs[:n], refs[n : 2 * n], refs[2 * n :]):
        c[...] = (a[...].astype(F32) + b[...].astype(F32)).astype(c.dtype)


def last_kernel(
    rows, where_ref, a_ref, a_got_ref, a_far_ref, a_row_ref, b_ref, b_got_ref, b_row_ref, b_far_ref, small_ref, *refs
):
    low, high = where_ref[0], where_ref[2]
    cut = a_ref.shape[1]
    own_ref, sends, turned_ref = refs[0], refs[1:-1], refs[-1]
    width = turned_ref.shape[0]
    turned_ref[...] = jnp.concatenate(
        [small_ref[...], jnp.zeros((PAD - 8, width), F32)], axis=0
    ).T

    def total(at, *parts):
        v = parts[0][at, :].astype(F32)
        for p in parts[1:]:
            v = v + p[at, :].astype(F32)
        return v

    for s, ref in enumerate((own_ref, *sends)):
        spot = high + s
        spot = jnp.where(spot >= len(sends) + 1, spot - len(sends) - 1, spot)
        at = pl.ds(pl.multiple_of(spot * rows, rows), rows)
        ref[:, :cut] = total(at, a_ref, a_got_ref, a_far_ref, a_row_ref).astype(ref.dtype)
        ref[:, cut : 2 * cut] = total(at, b_ref, b_got_ref, b_row_ref, b_far_ref).astype(ref.dtype)
        at = pl.ds(pl.multiple_of((2 * spot + low) * rows, rows), rows)
        ref[:, 2 * cut :] = turned_ref[at, :].astype(ref.dtype)


def mixer_input_kernel(
    rows,
    where_ref,
    tokens_ref,
    hidden_grad_ref,
    gains_ref,
    sums_ref,
    proj_ref,
    in_ref,
    input_ref,
    small_ref,
    grad_ref,
):
    width = tokens_ref.shape[1]
    step = 256
    inputs = tokens_ref[...].astype(F32)
    inverse = lax.rsqrt(jnp.mean(inputs * inputs, axis=1, keepdims=True) + EPSILON)

    def chunk(q, carry):
        at = pl.ds(q * step, step)
        grad_ref[:, at] = dot_last(proj_ref[...], in_ref[at, :])
        return carry

    for q in range(width // step):
        chunk(q, 0)
    grad = grad_ref[...]
    row = lax.broadcasted_iota(jnp.int32, (8, width), 0)
    gain_grad = jnp.sum(grad * (inputs * inverse), axis=0, keepdims=True)
    small_ref[...] = jnp.where(row == 0, gain_grad, sums_ref[...])
    weighted = grad * gains_ref[0:1, :]
    mean = jnp.mean(weighted * inputs, axis=1, keepdims=True)
    input_ref[...] = hidden_grad_ref[...] + inverse * (
        weighted - inputs * (inverse * inverse * mean)
    )


TILE = 256


def piece_specs(pieces, count, width):
    tiles = count // TILE
    return [
        pl.BlockSpec(
            (TILE, width), lambda t, k=k: (jnp.clip(t - k * tiles, 0, tiles - 1), 0)
        )
        for k in range(pieces)
    ]


def pick(refs, tiles):
    v = refs[0][...]
    for k in range(1, len(refs)):
        v = jnp.where(pl.program_id(0) >= k * tiles, refs[k][...], v)
    return v


def put_piece(refs, tiles, v):
    for k, ref in enumerate(refs):

        @pl.when((pl.program_id(0) >= k * tiles) & (pl.program_id(0) < (k + 1) * tiles))
        def _(ref=ref):
            ref[...] = v.astype(ref.dtype)


def whole_spec(v):
    return pl.BlockSpec(v.shape, lambda t: (0, 0))


def tiled(kernel, grid, in_specs, args, out_specs, outs, flops, limit=56, scratch=()):
    moved = sum(a.size * a.dtype.itemsize for a in args) + sum(
        o.size * jnp.dtype(o.dtype).itemsize for o in outs
    )
    return pl.pallas_call(
        kernel,
        grid=(grid,),
        in_specs=in_specs,
        out_specs=out_specs,
        out_shape=outs,
        scratch_shapes=list(scratch),
        compiler_params=pltpu.CompilerParams(vmem_limit_bytes=limit * MIB),
        cost_estimate=pl.CostEstimate(flops=flops, bytes_accessed=moved, transcendentals=0),
    )(*args)


def act_kernel(tiles, rows, where_ref, *refs):
    pieces, woven, (act_ref, silu_ref, slope_ref, gate_ref, up_ref) = refs[:4], refs[4:8], refs[8:]

    @pl.when(pl.program_id(0) == 0)
    def _():
        for k, whole_ref in enumerate((gate_ref, up_ref)):

            def put(to, at, ref, whole_ref=whole_ref):
                whole_ref[to, :] = ref[at, :]

            natural(where_ref[0], *woven[2 * k : 2 * k + 2], put, rows, woven[0].shape[0] // rows)

    normed = pick(pieces, tiles)
    gate = dot_plain(normed, gate_ref[...])
    up = dot_plain(normed, up_ref[...])
    sigmoid = 1.0 / (1.0 + jnp.exp(-gate))
    silu = gate * sigmoid
    act_ref[...] = (silu * up).astype(LINK)
    silu_ref[...] = silu.astype(LINK)
    slope_ref[...] = (up * (sigmoid + silu * (1.0 - sigmoid))).astype(LINK)


def act_call(rows, scalars, pieces, woven):
    count, width = pieces[0].shape
    inner = woven[0].shape[1]
    tiles = count // TILE
    wide = pl.BlockSpec((TILE, inner), lambda t: (t, 0))
    weight = shape((width, inner), LINK)
    return tiled(
        functools.partial(act_kernel, tiles, rows),
        4 * tiles,
        [SCALARS] + piece_specs(4, count, width) + [whole_spec(v) for v in woven],
        [scalars, *pieces, *woven],
        [wide] * 3 + [whole_spec(weight)] * 2,
        [shape((4 * count, inner), LINK)] * 3 + [weight] * 2,
        16 * count * width * inner,
    )


def back_kernel(pieces, tiles, with_got, *refs):
    cots, refs = refs[:pieces], refs[pieces:]
    silu_ref, slope_ref, gate_ref, up_ref, down_ref = refs[:5]
    refs = refs[5:]
    if with_got:
        got_ref, refs = refs[0], refs[1:]
    grad_gate_ref, grad_up_ref = refs[:2]
    grad_act = dot_plain(pick(cots, tiles), down_ref[...])
    grad_up_ref[...] = (grad_act * silu_ref[...].astype(F32)).astype(LINK)
    grad_gate_ref[...] = (grad_act * slope_ref[...].astype(F32)).astype(LINK)
    back = dot_last(grad_gate_ref[...], gate_ref[...]) + dot_last(grad_up_ref[...], up_ref[...])
    if with_got:
        back = back + got_ref[...].astype(F32)
    put_piece(refs[2:], tiles, back)


def back_call(start, cots, silu, slope, gate, up, down, got=None):
    count, width = cots[0].shape
    inner = gate.shape[1]
    tiles, pieces = count // TILE, len(cots)
    wide_in = pl.BlockSpec((TILE, inner), lambda t: (t + start * tiles, 0))
    wide = pl.BlockSpec((TILE, inner), lambda t: (t, 0))
    thin = piece_specs(pieces, count, width)
    extra = [] if got is None else [got]
    return tiled(
        functools.partial(back_kernel, pieces, tiles, got is not None),
        pieces * tiles,
        thin + [wide_in] * 2 + [whole_spec(gate)] * 3 + thin[: len(extra)],
        [*cots, silu, slope, gate, up, down, *extra],
        [wide] * 2 + thin,
        [shape((pieces * count, inner), LINK)] * 2 + [shape((count, width), LINK)] * pieces,
        6 * pieces * count * width * inner,
    )


def out_kernel(tiles, skip, act_ref, down_ref, *refs):
    put_piece(refs[skip:], tiles, dot_last(act_ref[...], down_ref[...]))


def out_call(act, down, count, deps):
    width, inner = down.shape
    tiles = count // TILE
    return tiled(
        functools.partial(out_kernel, tiles, len(deps)),
        4 * tiles,
        [pl.BlockSpec((TILE, inner), lambda t: (t, 0)), whole_spec(down)] + [APART] * len(deps),
        [act, down, *deps],
        piece_specs(4, count, width),
        [shape((count, width), LINK)] * 4,
        8 * count * width * inner,
    )


def weight_grad_kernel(rows, spots, whole, where_ref, *refs):
    lefts, refs = refs[:4], refs[4:]
    low = where_ref[0]
    count = lefts[0].shape[0]
    at = pl.ds(pl.multiple_of(pl.program_id(0) * TILE, TILE), TILE)
    total = None
    for left, (k, start) in zip(lefts, spots):
        v = dot_rows(left[:, at], refs[k][start * count : (start + 1) * count, :])
        total = v if total is None else total + v
    if whole:
        refs[-1][...] = total.astype(LINK)
        return
    near_ref, away_ref, total_ref = refs[-3:]
    total_ref[...] = total
    for h in range(near_ref.shape[0] // rows):
        to = pl.ds(h * rows, rows)
        for ref, bit in ((near_ref, low), (away_ref, 1 - low)):
            at = pl.ds(pl.multiple_of((2 * h + bit) * rows, rows), rows)
            ref[to, :] = total_ref[at, :].astype(ref.dtype)


def pair_grad_kernel(rows, spots, where_ref, *refs):
    lefts, gates, ups = refs[:4], refs[4:7], refs[7:10]
    near_ref, away_ref, up_ref, total_ref = refs[10:]
    low = where_ref[0]
    count = lefts[0].shape[0]
    at = pl.ds(pl.multiple_of(pl.program_id(0) * TILE, TILE), TILE)

    def total(rights):
        v = None
        for left, (k, start) in zip(lefts, spots):
            part = dot_rows(left[:, at], rights[k][start * count : (start + 1) * count, :])
            v = part if v is None else v + part
        return v

    up_ref[...] = total(ups).astype(LINK)
    total_ref[...] = total(gates)
    for h in range(near_ref.shape[0] // rows):
        to = pl.ds(h * rows, rows)
        for ref, bit in ((near_ref, low), (away_ref, 1 - low)):
            at_rows = pl.ds(pl.multiple_of((2 * h + bit) * rows, rows), rows)
            ref[to, :] = total_ref[at_rows, :].astype(ref.dtype)


def pair_grad(rows, scalars, lefts, gates, ups, spots):
    count, width = lefts[0].shape
    inner = gates[0].shape[1]
    half = pl.BlockSpec((TILE // 2, inner), lambda t: (t, 0))
    args = [*lefts, *gates, *ups]
    return tiled(
        functools.partial(pair_grad_kernel, rows, spots),
        width // TILE,
        [SCALARS] + [whole_spec(v) for v in args],
        [scalars, *args],
        [half, half, pl.BlockSpec((TILE, inner), lambda t: (t, 0))],
        [
            shape((width // 2, inner), F32),
            shape((width // 2, inner), LINK),
            shape((width, inner), LINK),
        ],
        16 * count * width * inner,
        scratch=[pltpu.VMEM((TILE, inner), F32)],
    )


def weight_grad(rows, scalars, lefts, rights, spots, whole=False):
    count, width = lefts[0].shape
    inner = rights[0].shape[1]
    half = pl.BlockSpec((TILE // 2, inner), lambda t: (t, 0))
    return tiled(
        functools.partial(weight_grad_kernel, rows, spots, whole),
        width // TILE,
        [SCALARS] + [whole_spec(v) for v in (*lefts, *rights)],
        [scalars, *lefts, *rights],
        [pl.BlockSpec((TILE, inner), lambda t: (t, 0))] if whole else [half, half],
        [shape((width, inner), LINK)]
        if whole
        else [shape((width // 2, inner), F32), shape((width // 2, inner), LINK)],
        8 * count * width * inner,
        scratch=[] if whole else [pltpu.VMEM((TILE, inner), F32)],
    )


def body(
    tokens,
    segments,
    mixer_gain,
    in_weight,
    conv_kernel,
    out_weight,
    ffn_gain,
    gate_weight,
    up_weight,
    down_weight,
    cotangent,
):
    count, width = tokens.shape
    rows = in_weight.shape[0]
    in_cols, out_cols = in_weight.shape[1], out_weight.shape[1]
    cut = (in_cols + out_cols) // 2
    ways = width // rows
    half = ways // 2
    columns = lax.axis_size("dp")
    place = lax.axis_index("dp")
    low = lax.rem(lax.axis_index("fsdp"), 2)
    high = lax.axis_index("fsdp") // 2
    scalars = jnp.stack([low, place, high]).astype(jnp.int32)
    strides = [[2 * h + bit for h in range(half)] for bit in range(2)]

    def swap_row(v):
        return lax.ppermute(v, "fsdp", [(i, i ^ 1) for i in range(ways)])

    def swap_far(v):
        return lax.ppermute(v, "dp", [(i, i ^ 2) for i in range(columns)])

    def swap_core(v):
        return lax.ppermute(v, "dp", [(i, i ^ 1) for i in range(columns)])

    def shift_high(v, s):
        return lax.ppermute(v, "fsdp", [(i, (i + 2 * s) % ways) for i in range(ways)])

    def gather_high(v):
        return lax.all_gather(v, "fsdp", axis=0, tiled=True, axis_index_groups=strides)

    def scatter_high(v):
        return lax.psum_scatter(
            v, "fsdp", scatter_dimension=0, tiled=True, axis_index_groups=strides
        )

    (packed,) = call(
        pack_kernel,
        scalars,
        [in_weight, out_weight, mixer_gain[None, :], ffn_gain[None, :], conv_kernel],
        [shape((rows, 2 * cut + PAD), LINK)],
    )
    shifts = [packed] + [shift_high(packed, s) for s in range(1, half)]
    tall = half * rows
    down_other = swap_row(after(down_weight, packed))
    down_pair = jnp.where(
        low == 0,
        jnp.concatenate([down_weight, down_other], axis=0),
        jnp.concatenate([down_other, down_weight], axis=0),
    )
    shifts[0] = after(shifts[0], down_pair)
    first, second, small_near = call(
        merge_kernel,
        scalars,
        shifts,
        [shape((tall, cut), LINK), shape((tall, cut), LINK), shape((tall, PAD), LINK)],
    )
    gate_near = gather_high(after(gate_weight, first))
    up_near = gather_high(after(up_weight, first))
    down_all = gather_high(after(down_pair, first))
    first_row = swap_row(first)
    second_far = swap_far(second)
    small_away = swap_row(small_near)
    second_row = swap_row(second)
    first_far = swap_far(first)
    second_far_row = swap_row(second_far)
    first_row_far = swap_far(first_row)
    cot_far = swap_far(after(cotangent, first_row_far))
    chip = [[[first, first_row], [first_far, first_row_far]], [[second, second_row], [second_far, second_far_row]]]
    pieces = []
    for k in range(2):
        other = [[swap_core(v) for v in pair] for pair in chip[k]]
        for pair in (chip[k][0], other[0], chip[k][1], other[1]):
            pieces += pair
    pieces[0] = after(pieces[0], gate_near, small_away)
    gate_row = swap_row(gate_near)
    up_row = swap_row(up_near)

    def gather_tokens(v, far):
        return [v, swap_core(v), far, swap_core(far)]

    cots = gather_tokens(cotangent, cot_far)

    seg_ids = segments[0]
    zero = jnp.zeros((2,), F32)
    same = jnp.stack(
        [
            jnp.concatenate([zero[:1], (seg_ids[1:] == seg_ids[:-1]).astype(F32)]),
            jnp.concatenate([zero, (seg_ids[2:] == seg_ids[:-2]).astype(F32)]),
        ],
        axis=1,
    )
    normed, parts, scaled, hidden, normed_two, gains, in_all, outw_all = call(
        functools.partial(mixer_kernel, rows),
        scalars,
        [tokens, same, small_near, small_away, *pieces],
        [
            shape((count, width), LINK),
            shape((3, count, width), F32),
            shape((count, width), LINK),
            shape((count, width), F32),
            shape((count, width), LINK),
            shape((8, width), F32),
            shape((width, columns * in_cols), LINK),
            shape((width, columns * out_cols), LINK),
        ],
        apart=2,
        flops=8 * count * width * width,
        scratch=[
            pltpu.VMEM((width, PAD), F32),
            pltpu.VMEM((width, columns * in_cols), LINK),
            pltpu.VMEM((width, columns * out_cols), LINK),
            pltpu.SemaphoreType.DMA,
            pltpu.SemaphoreType.DMA,
        ],
        limit=56,
    )

    normed_two = after(normed_two, up_near, cot_far, gate_row)
    normeds = gather_tokens(normed_two, swap_far(normed_two))
    act, silu, slope, gate_all, up_all = act_call(
        rows, scalars, normeds, [gate_near, gate_row, up_near, up_row]
    )

    def add(*pairs):
        return call(
            add_kernel,
            scalars,
            [p[0] for p in pairs] + [p[1] for p in pairs],
            [shape(p[0].shape, LINK) for p in pairs],
        )

    def join(near, away_got):
        return call(add_kernel, scalars, [near, away_got], [shape(near.shape, LINK)])[0]

    weights = (silu, slope, gate_all, up_all, down_all)
    gate_xc, up_xc, back_xc = back_call(3, [cots[3]], *weights)
    down_near, down_away = weight_grad(
        rows,
        scalars,
        [after(cots[0], back_xc), *cots[1:]],
        [act],
        [(0, 0), (0, 1), (0, 2), (0, 3)],
    )
    gate_x, up_x, back_far = back_call(
        2, [after(cots[2], down_away)], *weights, got=swap_core(back_xc)
    )
    gate_o, up_o, back_own, back_c = back_call(
        0, [after(cots[0], back_far), cots[1]], *weights
    )
    down_got = swap_row(down_away)
    back_one = swap_far(back_far[: 3 * count // 4])
    back_two = swap_far(back_far[3 * count // 4 :])
    spots = [(0, 0), (0, 1), (1, 0), (2, 0)]
    down_sum = join(down_near, down_got)
    gate_near_grad, gate_away, up_whole = pair_grad(
        rows,
        scalars,
        [after(normeds[0], down_sum, back_one), *normeds[1:]],
        [gate_o, gate_x, gate_xc],
        [up_o, up_x, up_xc],
        spots,
    )
    up_pair = scatter_high(up_whole).reshape(2, rows, -1)
    up_mine = jnp.where(low == 0, up_pair[0], up_pair[1])
    up_other = jnp.where(low == 0, up_pair[1], up_pair[0])
    grad_down = scatter_high(down_sum).astype(F32)
    gate_one = swap_row(gate_away[: tall // 2])
    gate_two = swap_row(gate_away[tall // 2 :])

    hidden_grad, branch, proj, sums = call(
        mixer_back_kernel,
        scalars,
        [after(back_own, gate_away), swap_core(back_c), back_one, back_two, hidden, cotangent, same, gains, parts, outw_all],
        [
            shape((count, width), F32),
            shape((count, width), LINK),
            shape((count, 3 * width), LINK),
            shape((8, width), F32),
        ],
        flops=2 * count * width * width,
        limit=48,
    )

    def mixer_grads(order, first_arg):
        return call(
            functools.partial(mixer_grads_kernel, rows, order),
            scalars,
            [first_arg, proj, branch, scaled],
            [shape((tall, cut), LINK)] * 8,
            flops=4 * count * width * width,
            scratch=[
                pltpu.VMEM((width, cut), F32),
                pltpu.VMEM((8, tall, cut), LINK),
                pltpu.SemaphoreType.DMA((8,)),
            ],
            apart=8,
        )

    input_grad, sums = call(
        functools.partial(mixer_input_kernel, rows),
        scalars,
        [tokens, hidden_grad, gains, sums, proj, in_all],
        [shape((count, width), F32), shape((8, width), F32)],
        flops=6 * count * width * width,
        scratch=[pltpu.VMEM((count, width), F32)],
    )
    sums_core = sums + swap_core(sums)
    sums_far = sums_core + swap_far(sums_core)
    send = mixer_grads((1, 3), after(normed, gate_one, input_grad))
    got = [swap_core(v) for v in send]
    mine = mixer_grads((0, 2), after(normed, send[0], sums_core))
    mine = [*mine[:5], after(mine[5], sums_far), *mine[6:]]
    a_away_far, b_away_far, a_near_far, b_away_own = add(
        *((after(mine[k], gate_two), got[k]) for k in (5, 7, 4, 3))
    )
    a_away_got = swap_far(a_away_far)
    b_away_got = swap_row(b_away_far)
    a_near_got = swap_far(a_near_far)
    b_own_got = swap_row(b_away_own)

    out_own, out_c, out_x, out_xc = out_call(after(act, a_near_far), down_all, count, [up_pair])
    gate_got = jnp.concatenate([gate_one, gate_two], axis=0)
    gate_sum = join(after(gate_near_grad, out_own), gate_got)
    grad_gate = scatter_high(gate_sum).astype(F32)
    a_away, b_far = call(
        join_kernel,
        scalars,
        [mine[1], got[1], a_away_got, mine[6], got[6], b_away_got],
        [shape((tall, cut), LINK)] * 2,
        deps=[out_own, a_near_got, b_own_got],
    )
    own, *sends = call(
        functools.partial(last_kernel, rows),
        scalars,
        [
            mine[0],
            got[0],
            a_near_got,
            swap_row(a_away),
            mine[2],
            got[2],
            b_own_got,
            swap_far(b_far),
            sums_far + swap_row(sums_far),
        ],
        [shape((rows, 2 * cut + PAD), F32)] + [shape((rows, 2 * cut + PAD), LINK)] * (half - 1),
        scratch=[pltpu.VMEM((width, PAD), F32)],
        deps=[gate_sum],
    )
    gots = [shift_high(sends[s - 1], s) for s in range(1, half)]
    (out_far,) = add((after(out_x, own), swap_core(out_xc)))
    out_got, out_got_far = swap_core(out_c), swap_far(out_far)
    up_row = swap_row(after(up_other, own))
    grad_up = up_mine.astype(F32) + up_row.astype(F32)
    grad_in, grad_outw, one_grad, two_grad, taps_grad = call(
        final_kernel,
        scalars,
        [own, *gots],
        [
            shape((rows, in_cols), F32),
            shape((rows, out_cols), F32),
            shape((1, rows), F32),
            shape((1, rows), F32),
            shape((rows, 3), F32),
        ],
        deps=[grad_up, grad_gate, grad_down],
    )
    result = (
        hidden + (out_own.astype(F32) + out_got.astype(F32) + out_got_far.astype(F32))
    ).astype(LINK)
    return (
        result,
        input_grad,
        one_grad[0],
        grad_in,
        taps_grad,
        grad_outw,
        two_grad[0],
        grad_gate,
        grad_up,
        grad_down,
    )


def solution(mesh):
    rows_spec, cols_spec = P(("dp", "fsdp"), None), P("fsdp", "dp")
    gain_spec, taps_spec = P("fsdp"), P("fsdp", None)
    return jax.shard_map(
        body,
        mesh=mesh,
        in_specs=(
            rows_spec,
            rows_spec,
            gain_spec,
            cols_spec,
            taps_spec,
            cols_spec,
            gain_spec,
            cols_spec,
            cols_spec,
            cols_spec,
            rows_spec,
        ),
        out_specs=(
            rows_spec,
            rows_spec,
            gain_spec,
            cols_spec,
            taps_spec,
            cols_spec,
            gain_spec,
            cols_spec,
            cols_spec,
            cols_spec,
        ),
        check_vma=False,
    )
```

profile of v0, /device:TPU:9, one launch (start us, length us, event | category | flops | bytes accessed | tf_op | source)
XLA Modules:
  0.0 380.0 jit_solution(11372265499196616102)
XLA Ops:
  22.2 12.2 %collective-permute-done.2.refs_3_ = bf16[128,1152]{1,0:T(8,128)(2,1)S(1)} collective-permute-done((bf16[128,1152]{1,0:T(8,128)(2,1)S(1)}, bf16[128,1152]{1,0:T(8,128)(2,1)S(1)}, u32[]{:S(2)}, u32[]{:S(2)}) %collective-permute-start.2) | collective-permute-done | bytes 294944 | tf_op jit(solution)/shard_map/ppermute | solution.py:645
  34.4 6.3 %collective-permute-done.1.refs_2_ = bf16[128,1152]{1,0:T(8,128)(2,1)S(1)} collective-permute-done((bf16[128,1152]{1,0:T(8,128)(2,1)S(1)}, bf16[128,1152]{1,0:T(8,128)(2,1)S(1)}, u32[]{:S(2)}, u32[]{:S(2)}) %collective-permute-start.1) | collective-permute-done | bytes 294944 | tf_op jit(solution)/shard_map/ppermute | solution.py:645
  46.7 10.9 %collective-permute-done.4.refs_4_ = bf16[512,128]{1,0:T(8,128)(2,1)S(1)} collective-permute-done((bf16[512,128]{1,0:T(8,128)(2,1)S(1)}, bf16[512,128]{1,0:T(8,128)(2,1)S(1)}, u32[]{:S(2)}, u32[]{:S(2)}) %collective-permute-start.4) | collective-permute-done | bytes 131104 | tf_op jit(solution)/shard_map/ppermute | solution.py:636
  58.5 4.2 %collective-permute-start.6 = (bf16[512,512]{1,0:T(8,128)(2,1)S(1)}, bf16[512,512]{1,0:T(8,128)(2,1)S(1)}, u32[]{:S(2)}, u32[]{:S(2)}) collective-permute-start(bf16[512,512]{1,0:T(8,128)(2,1)S(1)} %get-tuple-element.111.refs_5_), channel_id=1, source_target_pairs={{0,8},{8,0},{16,24},{24,16},{1,9},{9,1},{17,25},{25,17},{2,10},{10... | collective-permute-start | bytes 1572872 | tf_op jit(solution)/shard_map/ppermute | solution.py:642
  64.2 4.6 %collective-permute-done.12.refs_14_ = bf16[512,512]{1,0:T(8,128)(2,1)} collective-permute-done((bf16[512,512]{1,0:T(8,128)(2,1)S(1)}, bf16[512,512]{1,0:T(8,128)(2,1)}, u32[]{:S(2)}, u32[]{:S(2)}) %collective-permute-start.12) | collective-permute-done | bytes 524320 | tf_op jit(solution)/shard_map/ppermute | solution.py:636
  69.1 8.0 %collective-permute-start.14 = (bf16[512,512]{1,0:T(8,128)(2,1)}, bf16[512,512]{1,0:T(8,128)(2,1)}, u32[]{:S(2)}, u32[]{:S(2)}) collective-permute-start(bf16[512,512]{1,0:T(8,128)(2,1)} %collective-permute-done.12.refs_14_), channel_id=1, source_target_pairs={{0,8},{8,0},{16,24},{24,16},{1,9},{9,1},{17,25},{25,17},{2,10},{10... | collective-permute-start | bytes 1572872 | tf_op jit(solution)/shard_map/ppermute | solution.py:642
  80.1 5.7 %collective-permute-start.7 = (bf16[512,512]{1,0:T(8,128)(2,1)}, bf16[512,512]{1,0:T(8,128)(2,1)}, u32[]{:S(2)}, u32[]{:S(2)}) collective-permute-start(bf16[512,512]{1,0:T(8,128)(2,1)} %copy-done.61), channel_id=1, source_target_pairs={{0,8},{8,0},{16,24},{24,16},{1,9},{9,1},{17,25},{25,17},{2,10},{10... | collective-permute-start | bytes 1572872 | tf_op jit(solution)/shard_map/ppermute | solution.py:642
  89.3 15.0 %shard_map.188 = (bf16[512,1024]{1,0:T(8,128)(2,1)}, f32[3,512,1024]{2,1,0:T(8,128)}, bf16[512,1024]{1,0:T(8,128)(2,1)}, f32[512,1024]{1,0:T(8,128)}, bf16[512,1...) custom-call(s32[3]{0:T(128)} %copy-done.35, ...), custom_call_target="tpu_custom_call" | custom-call | flops 4294967296 | bytes 29659136 | tf_op jit(solution)/shard_map/pallas_call | solution.py:51
  110.5 14.3 %collective-permute-done.22.refs_2_ = bf16[512,1024]{1,0:T(8,128)(2,1)S(1)} collective-permute-done((bf16[512,1024]{1,0:T(8,128)(2,1)}, bf16[512,1024]{1,0:T(8,128)(2,1)S(1)}, u32[]{:S(2)}, u32[]{:S(2)}) %collective-permute-start.22) | collective-permute-done | bytes 1048608 | tf_op jit(solution)/shard_map/ppermute | solution.py:639
  124.8 5.3 %collective-permute-start.23 = (bf16[512,1024]{1,0:T(8,128)(2,1)S(1)}, bf16[512,1024]{1,0:T(8,128)(2,1)S(1)}, u32[]{:S(2)}, u32[]{:S(2)}) collective-permute-start(bf16[512,1024]{1,0:T(8,128)(2,1)S(1)} %collective-permute-done.22.refs_2_), channel_id=1, source_target_pairs={{0,8},{8,0},{16,24},{24,16},{1,9},{9,1},{17,25},{25,17},{2,10},{10... | collective-permute-start | bytes 3145736 | tf_op jit(solution)/shard_map/ppermute | solution.py:642
  133.4 18.5 %shard_map.189 = (bf16[2048,1152]{1,0:T(8,128)(2,1)}, bf16[2048,1152]{1,0:T(8,128)(2,1)}, bf16[2048,1152]{1,0:T(8,128)(2,1)}, bf16[1024,1152]{1,0:T(8,128)(2,1)}, bf16[1024,1152]{1,0:T(8,128)(2,1)}) custom-call(s32[3]{0:T(128)} %copy-done.35, bf16[512,1024]{1,0:T(8,128)(2,1)} %get-tuple-element.131.refs_0_, bf16[512,1024]{1,0:T(8,128)(2,1)} %copy-done.59, ...), custom_call_target="tpu_custom_call" | custom-call | flops 9663676416 | bytes 27787276 | tf_op jit(solution)/shard_map/pallas_call | solution.py:422
  153.9 9.6 %shard_map.190 = (bf16[512,1152]{1,0:T(8,128)(2,1)}, bf16[512,1152]{1,0:T(8,128)(2,1)}, bf16[512,1024]{1,0:T(8,128)(2,1)}) custom-call(bf16[512,1024]{1,0:T(8,128)(2,1)} %copy-done.50, bf16[2048,1152]{1,0:T(8,128)(2,1)} %get-tuple-element.120.refs_1_.refs_2_, bf16[2048,1152]{1,0:T(8,128)(2,1)} %get-tuple-element.121.refs_2_.refs_3_, ...), custom_call_target="tpu_custom_call" | custom-call | flops 3623878656 | bytes 20971520 | tf_op jit(solution)/shard_map/pallas_call | solution.py:422
  165.7 11.2 %shard_map.191 = (f32[512,1152]{1,0:T(8,128)}, bf16[512,1152]{1,0:T(8,128)(2,1)}) custom-call(s32[3]{0:T(128)} %copy-done.35, bf16[512,1024]{1,0:T(8,128)(2,1)} %refs_6_.1, bf16[512,1024]{1,0:T(8,128)(2,1)} %collective-permute-done.26.refs_1_, bf16[512,1024]{1,0:T(8,128)(2,1)} %copy-done.49, bf16[512,1024]{1,0:T(8,128)(2,1)} %copy-done.50, ...), custom_call_target="tpu_custom_call" | custom-call | flops 4831838208 | bytes 12451852 | tf_op jit(solution)/shard_map/pallas_call | solution.py:422
  179.3 10.0 %shard_map.193 = (bf16[512,1152]{1,0:T(8,128)(2,1)}, bf16[512,1152]{1,0:T(8,128)(2,1)}, bf16[512,1024]{1,0:T(8,128)(2,1)}) custom-call(bf16[512,1024]{1,0:T(8,128)(2,1)} %copy-done.49, bf16[2048,1152]{1,0:T(8,128)(2,1)} %get-tuple-element.120.refs_1_.refs_2_, bf16[2048,1152]{1,0:T(8,128)(2,1)} %get-tuple-element.121.refs_2_.refs_3_, ...), custom_call_target="tpu_custom_call" | custom-call | flops 3623878656 | bytes 22020096 | tf_op jit(solution)/shard_map/pallas_call | solution.py:422
  191.0 14.7 %shard_map.194 = (bf16[1024,1152]{1,0:T(8,128)(2,1)}, bf16[1024,1152]{1,0:T(8,128)(2,1)}, bf16[512,1024]{1,0:T(8,128)(2,1)}, bf16[512,1024]{1,0:T(8,128)(2,1)}) custom-call(bf16[512,1024]{1,0:T(8,128)(2,1)} %refs_6_.1, bf16[512,1024]{1,0:T(8,128)(2,1)} %collective-permute-done.26.refs_1_, bf16[2048,1152]{1,0:T(8,128)(2,1)} %get-tuple-element.120.refs_1_.refs_2_, ...), custom_call_target="tpu_custom_call" | custom-call | flops 7247757312 | bytes 25427968 | tf_op jit(solution)/shard_map/pallas_call | solution.py:422
  209.4 18.5 %shard_map.195 = (f32[512,1152]{1,0:T(8,128)}, bf16[512,1152]{1,0:T(8,128)(2,1)}, bf16[1024,1152]{1,0:T(8,128)(2,1)}) custom-call(s32[3]{0:T(128)} %copy-done.35, bf16[512,1024]{1,0:T(8,128)(2,1)} %get-tuple-element.131.refs_0_, bf16[512,1024]{1,0:T(8,128)(2,1)} %copy-done.59, bf16[512,1024]{1,0:T(8,128)(2,1)} %copy-done.58, bf16[512,1024]{1,0:T(8,128)(2,1)} %copy-done.60, ...), custom_call_target="tpu_custom_call" | custom-call | flops 9663676416 | bytes 19529740 | tf_op jit(solution)/shard_map/pallas_call | solution.py:422
  242.8 10.9 %shard_map.196 = (f32[512,1024]{1,0:T(8,128)}, bf16[512,1024]{1,0:T(8,128)(2,1)S(1)}, bf16[512,3072]{1,0:T(8,128)(2,1)}, f32[8,1024]{1,0:T(8,128)S(1)}) custom-call(s32[3]{0:T(128)S(1)} %copy-done.37, bf16[512,1024]{1,0:T(8,128)(2,1)S(1)} %copy-done.13, bf16[512,1024]{1,0:T(8,128)(2,1)S(1)} %copy-done.15, bf16[384,1024]{1,0:T(8,128)(2,1)S(1)} %copy-done.18, ...), custom_call_target="tpu_custom_call" | custom-call | flops 1073741824 | bytes 21041152 | tf_op jit(solution)/shard_map/pallas_call | solution.py:51
  257.3 5.9 %shard_map.197 = (f32[512,1024]{1,0:T(8,128)}, f32[8,1024]{1,0:T(8,128)S(1)}) custom-call(s32[3]{0:T(128)S(1)} %copy-done.37, bf16[512,1024]{1,0:T(8,128)(2,1)S(1)} %copy-done.12, f32[512,1024]{1,0:T(8,128)S(1)} %copy-done.8, f32[8,1024]{1,0:T(8,128)S(1)} %copy-done.34, f32[8,1024]{1,0:T(8,128)S(1)} %get-tuple-element.147.refs_4_, ...), custom_call_target="tpu_custom_call" | custom-call | flops 3221225472 | bytes 14778368 | tf_op jit(solution)/shard_map/pallas_call | solution.py:51
  263.2 6.8 %shard_map.198 = (bf16[512,512]{1,0:T(8,128)(2,1)S(1)}, bf16[512,512]{1,0:T(8,128)(2,1)S(1)}, bf16[512,512]{1,0:T(8,128)(2,1)S(1)}, bf16[512,512]{1,0:T(8,128)(2...) custom-call(s32[3]{0:T(128)S(1)} %copy-done.37, ...), custom_call_target="tpu_custom_call" | custom-call | flops 2147483648 | bytes 10485760 | tf_op jit(solution)/shard_map/pallas_call | solution.py:51
  278.9 6.6 %shard_map.199 = (bf16[512,512]{1,0:T(8,128)(2,1)S(1)}, bf16[512,512]{1,0:T(8,128)(2,1)S(1)}, bf16[512,512]{1,0:T(8,128)(2,1)S(1)}, bf16[512,512]{1,0:T(8,128)(2...) custom-call(s32[3]{0:T(128)S(1)} %copy-done.37, ...), custom_call_target="tpu_custom_call" | custom-call | flops 2147483648 | bytes 10485760 | tf_op jit(solution)/shard_map/pallas_call | solution.py:51
  291.7 12.1 %shard_map.201 = (bf16[512,1024]{1,0:T(8,128)(2,1)}, bf16[512,1024]{1,0:T(8,128)(2,1)}, bf16[512,1024]{1,0:T(8,128)(2,1)}, bf16[512,1024]{1,0:T(8,128)(2,1)}) custom-call(bf16[2048,1152]{1,0:T(8,128)(2,1)} %get-tuple-element.171.refs_4_.act_ref, bf16[1024,1152]{1,0:T(8,128)(2,1)} %all-gather.8.cloned.1.call-done.refs_5_.refs_6_.down_ref, ...), custom_call_target="tpu_custom_call" | custom-call | flops 4831838208 | bytes 11862016 | tf_op jit(solution)/shard_map/pallas_call | solution.py:422
  307.7 5.2 %collective-permute-done.44.refs_3_ = bf16[512,512]{1,0:T(8,128)(2,1)} collective-permute-done((bf16[512,512]{1,0:T(8,128)(2,1)}, bf16[512,512]{1,0:T(8,128)(2,1)}, u32[]{:S(2)}, u32[]{:S(2)}) %collective-permute-start.44) | collective-permute-done | bytes 524320 | tf_op jit(solution)/shard_map/ppermute | solution.py:639
  323.1 11.6 %collective-permute-done.48.refs_4_ = bf16[512,512]{1,0:T(8,128)(2,1)S(1)} collective-permute-done((bf16[512,512]{1,0:T(8,128)(2,1)S(1)}, bf16[512,512]{1,0:T(8,128)(2,1)S(1)}, u32[]{:S(2)}, u32[]{:S(2)}) %collective-permute-start.48) | collective-permute-done | bytes 524320 | tf_op jit(solution)/shard_map/ppermute | solution.py:636
  348.4 13.9 %collective-permute-done.53 = bf16[512,1024]{1,0:T(8,128)(2,1)} collective-permute-done((bf16[512,1024]{1,0:T(8,128)(2,1)}, bf16[512,1024]{1,0:T(8,128)(2,1)}, u32[]{:S(2)}, u32[]{:S(2)}) %collective-permute-start.53) | collective-permute-done | bytes 1048608 | tf_op jit(solution)/shard_map/ppermute | solution.py:639
  (291 shorter events, 122.9 us)
Async XLA Ops:
  7.2 70.7 %all-gather.4.cloned.1.call-start = ((), (), s32[]{:S(2)}) async-start(), calls=%async_computation.3 | async-start | bytes 1474560 | tf_op jit(solution)/shard_map/all_gather | solution.py:648
  15.8 24.9 %collective-permute-start.1 = (bf16[128,1152]{1,0:T(8,128)(2,1)S(1)}, bf16[128,1152]{1,0:T(8,128)(2,1)S(1)}, u32[]{:S(2)}, u32[]{:S(2)}) collective-permute-start(bf16[128,1152]{1,0:T(8,128)(2,1)S(1)} %shard_map.186.refs_1_), channel_id=1, source_target_pairs={{0,2},{1,3},{2,4},{3,5},{4,6},{5,7},{6,0},{7,1},{8,10},{9,11},{10,... | collective-permute-start | bytes 884744 | tf_op jit(solution)/shard_map/ppermute | solution.py:645
  41.4 62.8 %all-gather.6.cloned.1.call-start = ((), (), s32[]{:S(2)}) async-start(), calls=%async_computation.4 | async-start | bytes 1474560 | tf_op jit(solution)/shard_map/all_gather | solution.py:648
  42.8 111.1 %all-gather.8.cloned.1.call-start = ((), (), s32[]{:S(2)}) async-start(), calls=%async_computation.5 | async-start | bytes 2949120 | tf_op jit(solution)/shard_map/all_gather | solution.py:648
  77.9 26.3 %collective-permute-start.20 = (bf16[512,1152]{1,0:T(8,128)(2,1)}, bf16[512,1152]{1,0:T(8,128)(2,1)}, u32[]{:S(2)}, u32[]{:S(2)}) collective-permute-start(bf16[512,1152]{1,0:T(8,128)(2,1)} %all-gather.4.cloned.1.call-done.refs_4_), channel_id=1, source_target_pairs={{0,1},{1,0},{2,3},{3,2},{4,5},{5,4},{6,7},{7,6},{8,9},{9,8},{10,11... | collective-permute-start | bytes 3538952 | tf_op jit(solution)/shard_map/ppermute | solution.py:636
  78.2 26.0 %collective-permute-start.19 = (bf16[512,1024]{1,0:T(8,128)(2,1)S(1)}, bf16[512,1024]{1,0:T(8,128)(2,1)S(1)}, u32[]{:S(2)}, u32[]{:S(2)}) collective-permute-start(bf16[512,1024]{1,0:T(8,128)(2,1)S(1)} %copy-done.10), channel_id=1, source_target_pairs={{0,16},{8,24},{16,0},{24,8},{1,17},{9,25},{17,1},{25,9},{2,18},{10... | collective-permute-start | bytes 3145736 | tf_op jit(solution)/shard_map/ppermute | solution.py:639
  86.6 205.1 %reduce-scatter.4.cloned.1.call-start = ((), (), s32[]{:S(2)}) async-start(), calls=%async_computation.6 | async-start | bytes 2949120 | tf_op jit(solution)/shard_map/reduce_scatter | solution.py:651
  105.4 25.2 %collective-permute-start.24 = (bf16[512,1152]{1,0:T(8,128)(2,1)}, bf16[512,1152]{1,0:T(8,128)(2,1)S(1)}, u32[]{:S(2)}, u32[]{:S(2)}) collective-permute-start(bf16[512,1152]{1,0:T(8,128)(2,1)} %all-gather.6.cloned.1.call-done.refs_6_), channel_id=1, source_target_pairs={{0,1},{1,0},{2,3},{3,2},{4,5},{5,4},{6,7},{7,6},{8,9},{9,8},{10,11... | collective-permute-start | bytes 3538952 | tf_op jit(solution)/shard_map/ppermute | solution.py:636
  130.1 35.6 %collective-permute-start.26 = (bf16[512,1024]{1,0:T(8,128)(2,1)S(1)}, bf16[512,1024]{1,0:T(8,128)(2,1)}, u32[]{:S(2)}, u32[]{:S(2)}) collective-permute-start(bf16[512,1024]{1,0:T(8,128)(2,1)S(1)} %copy-done.10), channel_id=1, source_target_pairs={{0,8},{8,0},{16,24},{24,16},{1,9},{9,1},{17,25},{25,17},{2,10},{10... | collective-permute-start | bytes 3145736 | tf_op jit(solution)/shard_map/ppermute | solution.py:642
  176.9 28.8 %collective-permute-start.27 = (bf16[512,1152]{1,0:T(8,128)(2,1)}, bf16[512,1152]{1,0:T(8,128)(2,1)S(1)}, u32[]{:S(2)}, u32[]{:S(2)}) collective-permute-start(bf16[512,1152]{1,0:T(8,128)(2,1)} %get-tuple-element.128), channel_id=1, source_target_pairs={{0,1},{1,0},{2,3},{3,2},{4,5},{5,4},{6,7},{7,6},{8,9},{9,8},{10,11... | collective-permute-start | bytes 3538952 | tf_op jit(solution)/shard_map/ppermute | solution.py:636
  227.9 112.4 %reduce-scatter.8.cloned.1.call-start = ((), (), s32[]{:S(2)}) async-start(), calls=%async_computation.8 | async-start | bytes 1474560 | tf_op jit(solution)/shard_map/reduce_scatter | solution.py:651
  230.7 135.6 %reduce-scatter.6.cloned.1.call-start = ((), (), s32[]{:S(2)}) async-start(), calls=%async_computation.7 | async-start | bytes 1474560 | tf_op jit(solution)/shard_map/reduce_scatter | solution.py:651
  233.4 29.8 %collective-permute-start.30 = (bf16[256,1152]{1,0:T(8,128)(2,1)}, bf16[256,1152]{1,0:T(8,128)(2,1)S(1)}, u32[]{:S(2)}, u32[]{:S(2)}) collective-permute-start(bf16[256,1152]{1,0:T(8,128)(2,1)} %get-tuple-element.233), channel_id=1, source_target_pairs={{0,1},{1,0},{2,3},{3,2},{4,5},{5,4},{6,7},{7,6},{8,9},{9,8},{10,11... | collective-permute-start | bytes 1769480 | tf_op jit(solution)/shard_map/ppermute | solution.py:636
  233.6 44.6 %collective-permute-start.35 = (bf16[256,1152]{1,0:T(8,128)(2,1)S(1)}, bf16[256,1152]{1,0:T(8,128)(2,1)S(1)}, u32[]{:S(2)}, u32[]{:S(2)}) collective-permute-start(bf16[256,1152]{1,0:T(8,128)(2,1)S(1)} %get-tuple-element.232), channel_id=1, source_target_pairs={{0,1},{1,0},{2,3},{3,2},{4,5},{5,4},{6,7},{7,6},{8,9},{9,8},{10,11... | collective-permute-start | bytes 1769480 | tf_op jit(solution)/shard_map/ppermute | solution.py:636
  278.4 25.4 %collective-permute-start.45 = (bf16[512,512]{1,0:T(8,128)(2,1)S(1)}, bf16[512,512]{1,0:T(8,128)(2,1)S(1)}, u32[]{:S(2)}, u32[]{:S(2)}) collective-permute-start(bf16[512,512]{1,0:T(8,128)(2,1)S(1)} %get-tuple-element.181), channel_id=1, source_target_pairs={{0,8},{8,0},{16,24},{24,16},{1,9},{9,1},{17,25},{25,17},{2,10},{10... | collective-permute-start | bytes 1572872 | tf_op jit(solution)/shard_map/ppermute | solution.py:642
  287.9 27.3 %collective-permute-start.42 = (bf16[512,512]{1,0:T(8,128)(2,1)}, bf16[512,512]{1,0:T(8,128)(2,1)S(1)}, u32[]{:S(2)}, u32[]{:S(2)}) collective-permute-start(bf16[512,512]{1,0:T(8,128)(2,1)} %get-tuple-element.170), channel_id=1, source_target_pairs={{0,16},{8,24},{16,0},{24,8},{1,17},{9,25},{17,1},{25,9},{2,18},{10... | collective-permute-start | bytes 1572872 | tf_op jit(solution)/shard_map/ppermute | solution.py:639
  288.3 24.6 %collective-permute-start.44 = (bf16[512,512]{1,0:T(8,128)(2,1)}, bf16[512,512]{1,0:T(8,128)(2,1)}, u32[]{:S(2)}, u32[]{:S(2)}) collective-permute-start(bf16[512,512]{1,0:T(8,128)(2,1)} %get-tuple-element.179), channel_id=1, source_target_pairs={{0,16},{8,24},{16,0},{24,8},{1,17},{9,25},{17,1},{25,9},{2,18},{10... | collective-permute-start | bytes 1572872 | tf_op jit(solution)/shard_map/ppermute | solution.py:639
  290.2 23.9 %collective-permute-start.47 = (bf16[512,512]{1,0:T(8,128)(2,1)}, bf16[512,512]{1,0:T(8,128)(2,1)S(1)}, u32[]{:S(2)}, u32[]{:S(2)}) collective-permute-start(bf16[512,512]{1,0:T(8,128)(2,1)} %get-tuple-element.183), channel_id=1, source_target_pairs={{0,1},{1,0},{2,3},{3,2},{4,5},{5,4},{6,7},{7,6},{8,9},{9,8},{10,11... | collective-permute-start | bytes 1572872 | tf_op jit(solution)/shard_map/ppermute | solution.py:636
  304.6 32.2 %collective-permute-start.52 = (bf16[512,1024]{1,0:T(8,128)(2,1)}, bf16[512,1024]{1,0:T(8,128)(2,1)S(1)}, u32[]{:S(2)}, u32[]{:S(2)}) collective-permute-start(bf16[512,1024]{1,0:T(8,128)(2,1)} %get-tuple-element.192), channel_id=1, source_target_pairs={{0,8},{8,0},{16,24},{24,16},{1,9},{9,1},{17,25},{25,17},{2,10},{10... | collective-permute-start | bytes 3145736 | tf_op jit(solution)/shard_map/ppermute | solution.py:642
  322.0 26.4 %collective-permute-start.40 = (bf16[512,1024]{1,0:T(8,128)(2,1)}, bf16[512,1024]{1,0:T(8,128)(2,1)}, u32[]{:S(2)}, u32[]{:S(2)}) collective-permute-start(bf16[512,1024]{1,0:T(8,128)(2,1)} %get-tuple-element.174), channel_id=1, source_target_pairs={{0,8},{8,0},{16,24},{24,16},{1,9},{9,1},{17,25},{25,17},{2,10},{10... | collective-permute-start | bytes 3145736 | tf_op jit(solution)/shard_map/ppermute | solution.py:642
  338.6 23.7 %collective-permute-start.53 = (bf16[512,1024]{1,0:T(8,128)(2,1)}, bf16[512,1024]{1,0:T(8,128)(2,1)}, u32[]{:S(2)}, u32[]{:S(2)}) collective-permute-start(bf16[512,1024]{1,0:T(8,128)(2,1)} %shard_map.205), channel_id=1, source_target_pairs={{0,16},{8,24},{16,0},{24,8},{1,17},{9,25},{17,1},{25,9},{2,18},{10... | collective-permute-start | bytes 3145736 | tf_op jit(solution)/shard_map/ppermute | solution.py:639
  341.4 25.9 %collective-permute-start.54 = (bf16[128,1152]{1,0:T(8,128)(2,1)}, bf16[128,1152]{1,0:T(8,128)(2,1)S(1)}, u32[]{:S(2)}, u32[]{:S(2)}) collective-permute-start(bf16[128,1152]{1,0:T(8,128)(2,1)} %get-tuple-element.193), channel_id=1, source_target_pairs={{0,2},{1,3},{2,4},{3,5},{4,6},{5,7},{6,0},{7,1},{8,10},{9,11},{10,... | collective-permute-start | bytes 884744 | tf_op jit(solution)/shard_map/ppermute | solution.py:645
  343.4 24.0 %collective-permute-start.55 = (bf16[128,1152]{1,0:T(8,128)(2,1)}, bf16[128,1152]{1,0:T(8,128)(2,1)S(1)}, u32[]{:S(2)}, u32[]{:S(2)}) collective-permute-start(bf16[128,1152]{1,0:T(8,128)(2,1)} %get-tuple-element.194), channel_id=1, source_target_pairs={{0,4},{1,5},{2,6},{3,7},{4,0},{5,1},{6,2},{7,3},{8,12},{9,13},{10,... | collective-permute-start | bytes 884744 | tf_op jit(solution)/shard_map/ppermute | solution.py:645
  346.4 24.0 %collective-permute-start.56 = (bf16[128,1152]{1,0:T(8,128)(2,1)}, bf16[128,1152]{1,0:T(8,128)(2,1)}, u32[]{:S(2)}, u32[]{:S(2)}) collective-permute-start(bf16[128,1152]{1,0:T(8,128)(2,1)} %get-tuple-element.195), channel_id=1, source_target_pairs={{0,6},{1,7},{2,0},{3,1},{4,2},{5,3},{6,4},{7,5},{8,14},{9,15},{10,... | collective-permute-start | bytes 884744 | tf_op jit(solution)/shard_map/ppermute | solution.py:645
  (107 other events, 1349.9 us)
Sparse Core Ops, SparseCore 0:
  41.5 30.4 all-gather.3
  73.6 29.5 all-gather.5
  105.3 48.4 all-gather.7
  228.0 45.3 reduce-scatter.3
  275.5 29.0 reduce-scatter.7
  307.8 26.8 reduce-scatter.5
where the time goes:
time: 384 us; the launch traced here: 380 us
  Pallas kernels  154 us (40%)
  waiting for transfers between devices  101 us (26%)
  starting transfers between devices  72 us (19%)
  local copies, waits for them, and re-layouts  27.7 us (7%)
  between operations  15 us (4%)
  other arithmetic  10.3 us (3%)
    pallas_call x7, Pallas kernels, tiled(): pl.pallas_call(kernel, grid=(grid,), in_specs=in_specs, out_specs=out_spe...  94.6 us
    pallas_call x14, Pallas kernels, call(): pl.pallas_call(run, out_shape=outs, in_specs=[SCALARS] + [WHOLE] * len(ar...  59.8 us
    ppermute x25, starting transfers between devices, swap_core(): return lax.ppermute(v, 'dp', [(i, i ^ 1) for i in range(columns)])  41.3 us
    ppermute x12, waiting for transfers between devices, swap_far(): return lax.ppermute(v, 'dp', [(i, i ^ 2) for i in range(columns)])  40.5 us
    ppermute x15, waiting for transfers between devices, swap_row(): return lax.ppermute(v, 'fsdp', [(i, i ^ 1) for i in range(ways)])  31.7 us
    unnamed x136, local copies, waits for them, and re-layouts  23 us
    ppermute x6, waiting for transfers between devices, shift_high(): lax.ppermute(v, 'fsdp', [(i, (i + 2 * s) % ways) for i in range(ways)])  21.7 us
    ppermute x15, starting transfers between devices, swap_row(): return lax.ppermute(v, 'fsdp', [(i, i ^ 1) for i in range(ways)])  11.5 us
  transfers between devices with their start and end apart: 64, of which 21 were waited for; matrix products, arithmetic and copies ran while one was open for 4% of the time, Pallas kernels for 35%

commit v1 on v0

--- a/solution.py
+++ b/solution.py
@@ -309,9 +309,8 @@
 
 
 def join_kernel(where_ref, *refs):
-    for k in range(2):
-        a, b, c = (r[...].astype(F32) for r in refs[3 * k : 3 * k + 3])
-        refs[6 + k][...] = (a + b + c).astype(LINK)
+    a, b, c = (r[...].astype(F32) for r in refs[:3])
+    refs[3][...] = (a + b + c).astype(LINK)
 
 
 def add_kernel(where_ref, *refs):
@@ -838,16 +837,19 @@
     b_own_got = swap_row(b_away_own)
 
     out_own, out_c, out_x, out_xc = out_call(after(act, a_near_far), down_all, count, [up_pair])
+    (a_away,), (b_far,) = (
+        call(join_kernel, scalars, parts, [shape((tall, cut), LINK)], deps=[out_own])
+        for parts in ([mine[1], got[1], a_away_got], [mine[6], got[6], b_away_got])
+    )
     gate_got = jnp.concatenate([gate_one, gate_two], axis=0)
-    gate_sum = join(after(gate_near_grad, out_own), gate_got)
+    (gate_sum,) = call(
+        add_kernel,
+        scalars,
+        [gate_near_grad, gate_got],
+        [shape(gate_near_grad.shape, LINK)],
+        deps=[a_near_got, b_own_got, a_away, b_far],
+    )
     grad_gate = scatter_high(gate_sum).astype(F32)
-    a_away, b_far = call(
-        join_kernel,
-        scalars,
-        [mine[1], got[1], a_away_got, mine[6], got[6], b_away_got],
-        [shape((tall, cut), LINK)] * 2,
-        deps=[out_own, a_near_got, b_own_got],
-    )
     own, *sends = call(
         functools.partial(last_kernel, rows),
         scalars,

time: 384 us -> 383 us (level)
    ppermute x12, waiting for transfers between devices: 40.5 us -> 33.6 us  [swap_far(): return lax.ppermute(v, 'dp', [(i, i ^ 2) for i in range(columns)])]
    unnamed x136 -> x142, local copies, waits for them, and re-layouts: 23 us -> 24.1 us
    pallas_call x14 -> x15, Pallas kernels: 59.8 us -> 60.3 us  [call(): pl.pallas_call(run, out_shape=outs, in_specs=[SCALARS] + [WHOLE] * len(ar...]
  transfers between devices with their start and end apart: 64 -> 64, of which waited for: 21 -> 20; matrix products, arithmetic and copies ran while one was open for 4% -> 4% of each run, Pallas kernels for 35% -> 35%
where the time goes in v1:
time: 383 us; the launch traced here: 379 us
  Pallas kernels  155 us (40%)
  waiting for transfers between devices  98.6 us (26%)
  starting transfers between devices  72.9 us (19%)
  local copies, waits for them, and re-layouts  28.1 us (7%)
  between operations  15 us (4%)
  other arithmetic  9.94 us (3%)
    pallas_call x7, Pallas kernels, tiled(): pl.pallas_call(kernel, grid=(grid,), in_specs=in_specs, out_specs=out_spe...  94.6 us
    pallas_call x15, Pallas kernels, call(): pl.pallas_call(run, out_shape=outs, in_specs=[SCALARS] + [WHOLE] * len(ar...  60.3 us
    ppermute x25, starting transfers between devices, swap_core(): return lax.ppermute(v, 'dp', [(i, i ^ 1) for i in range(columns)])  41.6 us
    ppermute x15, waiting for transfers between devices, swap_row(): return lax.ppermute(v, 'fsdp', [(i, i ^ 1) for i in range(ways)])  35.4 us
    ppermute x12, waiting for transfers between devices, swap_far(): return lax.ppermute(v, 'dp', [(i, i ^ 2) for i in range(columns)])  33.6 us
    unnamed x142, local copies, waits for them, and re-layouts  24.1 us
    ppermute x6, waiting for transfers between devices, shift_high(): lax.ppermute(v, 'fsdp', [(i, (i + 2 * s) % ways) for i in range(ways)])  23.6 us
    ppermute x15, starting transfers between devices, swap_row(): return lax.ppermute(v, 'fsdp', [(i, i ^ 1) for i in range(ways)])  12.1 us
  transfers between devices with their start and end apart: 64, of which 20 were waited for; matrix products, arithmetic and copies ran while one was open for 4% of the time, Pallas kernels for 35%

profile of v1, /device:TPU:9, one launch (start us, length us, event | category | flops | bytes accessed | tf_op | source)
XLA Modules:
  0.0 379.4 jit_solution(12620221614861368594)
XLA Ops:
  22.2 12.2 %collective-permute-done.2.refs_3_ = bf16[128,1152]{1,0:T(8,128)(2,1)S(1)} collective-permute-done((bf16[128,1152]{1,0:T(8,128)(2,1)S(1)}, bf16[128,1152]{1,0:T(8,128)(2,1)S(1)}, u32[]{:S(2)}, u32[]{:S(2)}) %collective-permute-start.2) | collective-permute-done | bytes 294944 | tf_op jit(solution)/shard_map/ppermute | solution.py:644
  34.4 6.3 %collective-permute-done.1.refs_2_ = bf16[128,1152]{1,0:T(8,128)(2,1)S(1)} collective-permute-done((bf16[128,1152]{1,0:T(8,128)(2,1)S(1)}, bf16[128,1152]{1,0:T(8,128)(2,1)S(1)}, u32[]{:S(2)}, u32[]{:S(2)}) %collective-permute-start.1) | collective-permute-done | bytes 294944 | tf_op jit(solution)/shard_map/ppermute | solution.py:644
  46.7 10.9 %collective-permute-done.4.refs_4_ = bf16[512,128]{1,0:T(8,128)(2,1)S(1)} collective-permute-done((bf16[512,128]{1,0:T(8,128)(2,1)S(1)}, bf16[512,128]{1,0:T(8,128)(2,1)S(1)}, u32[]{:S(2)}, u32[]{:S(2)}) %collective-permute-start.4) | collective-permute-done | bytes 131104 | tf_op jit(solution)/shard_map/ppermute | solution.py:635
  58.5 4.2 %collective-permute-start.6 = (bf16[512,512]{1,0:T(8,128)(2,1)S(1)}, bf16[512,512]{1,0:T(8,128)(2,1)S(1)}, u32[]{:S(2)}, u32[]{:S(2)}) collective-permute-start(bf16[512,512]{1,0:T(8,128)(2,1)S(1)} %get-tuple-element.108.refs_5_), channel_id=1, source_target_pairs={{0,8},{8,0},{16,24},{24,16},{1,9},{9,1},{17,25},{25,17},{2,10},{10... | collective-permute-start | bytes 1572872 | tf_op jit(solution)/shard_map/ppermute | solution.py:641
  64.2 4.6 %collective-permute-done.12.refs_14_ = bf16[512,512]{1,0:T(8,128)(2,1)} collective-permute-done((bf16[512,512]{1,0:T(8,128)(2,1)S(1)}, bf16[512,512]{1,0:T(8,128)(2,1)}, u32[]{:S(2)}, u32[]{:S(2)}) %collective-permute-start.12) | collective-permute-done | bytes 524320 | tf_op jit(solution)/shard_map/ppermute | solution.py:635
  69.1 8.0 %collective-permute-start.14 = (bf16[512,512]{1,0:T(8,128)(2,1)}, bf16[512,512]{1,0:T(8,128)(2,1)}, u32[]{:S(2)}, u32[]{:S(2)}) collective-permute-start(bf16[512,512]{1,0:T(8,128)(2,1)} %collective-permute-done.12.refs_14_), channel_id=1, source_target_pairs={{0,8},{8,0},{16,24},{24,16},{1,9},{9,1},{17,25},{25,17},{2,10},{10... | collective-permute-start | bytes 1572872 | tf_op jit(solution)/shard_map/ppermute | solution.py:641
  80.1 5.7 %collective-permute-start.7 = (bf16[512,512]{1,0:T(8,128)(2,1)}, bf16[512,512]{1,0:T(8,128)(2,1)}, u32[]{:S(2)}, u32[]{:S(2)}) collective-permute-start(bf16[512,512]{1,0:T(8,128)(2,1)} %copy-done.64), channel_id=1, source_target_pairs={{0,8},{8,0},{16,24},{24,16},{1,9},{9,1},{17,25},{25,17},{2,10},{10... | collective-permute-start | bytes 1572872 | tf_op jit(solution)/shard_map/ppermute | solution.py:641
  89.3 15.0 %shard_map.188 = (bf16[512,1024]{1,0:T(8,128)(2,1)}, f32[3,512,1024]{2,1,0:T(8,128)}, bf16[512,1024]{1,0:T(8,128)(2,1)}, f32[512,1024]{1,0:T(8,128)}, bf16[512,1...) custom-call(s32[3]{0:T(128)} %copy-done.35, ...), custom_call_target="tpu_custom_call" | custom-call | flops 4294967296 | bytes 29659136 | tf_op jit(solution)/shard_map/pallas_call | solution.py:51
  110.5 14.4 %collective-permute-done.22.refs_2_ = bf16[512,1024]{1,0:T(8,128)(2,1)S(1)} collective-permute-done((bf16[512,1024]{1,0:T(8,128)(2,1)}, bf16[512,1024]{1,0:T(8,128)(2,1)S(1)}, u32[]{:S(2)}, u32[]{:S(2)}) %collective-permute-start.22) | collective-permute-done | bytes 1048608 | tf_op jit(solution)/shard_map/ppermute | solution.py:638
  124.9 5.3 %collective-permute-start.23 = (bf16[512,1024]{1,0:T(8,128)(2,1)S(1)}, bf16[512,1024]{1,0:T(8,128)(2,1)S(1)}, u32[]{:S(2)}, u32[]{:S(2)}) collective-permute-start(bf16[512,1024]{1,0:T(8,128)(2,1)S(1)} %collective-permute-done.22.refs_2_), channel_id=1, source_target_pairs={{0,8},{8,0},{16,24},{24,16},{1,9},{9,1},{17,25},{25,17},{2,10},{10... | collective-permute-start | bytes 3145736 | tf_op jit(solution)/shard_map/ppermute | solution.py:641
  133.4 18.5 %shard_map.189 = (bf16[2048,1152]{1,0:T(8,128)(2,1)}, bf16[2048,1152]{1,0:T(8,128)(2,1)}, bf16[2048,1152]{1,0:T(8,128)(2,1)}, bf16[1024,1152]{1,0:T(8,128)(2,1)}, bf16[1024,1152]{1,0:T(8,128)(2,1)}) custom-call(s32[3]{0:T(128)} %copy-done.35, bf16[512,1024]{1,0:T(8,128)(2,1)} %get-tuple-element.128.refs_0_, bf16[512,1024]{1,0:T(8,128)(2,1)} %copy-done.62, ...), custom_call_target="tpu_custom_call" | custom-call | flops 9663676416 | bytes 27787276 | tf_op jit(solution)/shard_map/pallas_call | solution.py:421
  153.9 9.6 %shard_map.190 = (bf16[512,1152]{1,0:T(8,128)(2,1)}, bf16[512,1152]{1,0:T(8,128)(2,1)}, bf16[512,1024]{1,0:T(8,128)(2,1)}) custom-call(bf16[512,1024]{1,0:T(8,128)(2,1)} %copy-done.52, bf16[2048,1152]{1,0:T(8,128)(2,1)} %get-tuple-element.117.refs_1_.refs_2_, bf16[2048,1152]{1,0:T(8,128)(2,1)} %get-tuple-element.118.refs_2_.refs_3_, ...), custom_call_target="tpu_custom_call" | custom-call | flops 3623878656 | bytes 20971520 | tf_op jit(solution)/shard_map/pallas_call | solution.py:421
  165.7 11.2 %shard_map.191 = (f32[512,1152]{1,0:T(8,128)}, bf16[512,1152]{1,0:T(8,128)(2,1)}) custom-call(s32[3]{0:T(128)} %copy-done.35, bf16[512,1024]{1,0:T(8,128)(2,1)} %refs_6_.1, bf16[512,1024]{1,0:T(8,128)(2,1)} %collective-permute-done.26.refs_1_, bf16[512,1024]{1,0:T(8,128)(2,1)} %copy-done.51, bf16[512,1024]{1,0:T(8,128)(2,1)} %copy-done.52, ...), custom_call_target="tpu_custom_call" | custom-call | flops 4831838208 | bytes 12451852 | tf_op jit(solution)/shard_map/pallas_call | solution.py:421
  179.3 10.0 %shard_map.193 = (bf16[512,1152]{1,0:T(8,128)(2,1)}, bf16[512,1152]{1,0:T(8,128)(2,1)}, bf16[512,1024]{1,0:T(8,128)(2,1)}) custom-call(bf16[512,1024]{1,0:T(8,128)(2,1)} %copy-done.51, bf16[2048,1152]{1,0:T(8,128)(2,1)} %get-tuple-element.117.refs_1_.refs_2_, bf16[2048,1152]{1,0:T(8,128)(2,1)} %get-tuple-element.118.refs_2_.refs_3_, ...), custom_call_target="tpu_custom_call" | custom-call | flops 3623878656 | bytes 22020096 | tf_op jit(solution)/shard_map/pallas_call | solution.py:421
  191.0 14.7 %shard_map.194 = (bf16[1024,1152]{1,0:T(8,128)(2,1)}, bf16[1024,1152]{1,0:T(8,128)(2,1)}, bf16[512,1024]{1,0:T(8,128)(2,1)}, bf16[512,1024]{1,0:T(8,128)(2,1)}) custom-call(bf16[512,1024]{1,0:T(8,128)(2,1)} %refs_6_.1, bf16[512,1024]{1,0:T(8,128)(2,1)} %collective-permute-done.26.refs_1_, bf16[2048,1152]{1,0:T(8,128)(2,1)} %get-tuple-element.117.refs_1_.refs_2_, ...), custom_call_target="tpu_custom_call" | custom-call | flops 7247757312 | bytes 25427968 | tf_op jit(solution)/shard_map/pallas_call | solution.py:421
  209.4 18.5 %shard_map.195 = (f32[512,1152]{1,0:T(8,128)}, bf16[512,1152]{1,0:T(8,128)(2,1)}, bf16[1024,1152]{1,0:T(8,128)(2,1)}) custom-call(s32[3]{0:T(128)} %copy-done.35, bf16[512,1024]{1,0:T(8,128)(2,1)} %get-tuple-element.128.refs_0_, bf16[512,1024]{1,0:T(8,128)(2,1)} %copy-done.62, bf16[512,1024]{1,0:T(8,128)(2,1)} %copy-done.61, bf16[512,1024]{1,0:T(8,128)(2,1)} %copy-done.63, ...), custom_call_target="tpu_custom_call" | custom-call | flops 9663676416 | bytes 19529740 | tf_op jit(solution)/shard_map/pallas_call | solution.py:421
  242.8 11.0 %shard_map.196 = (f32[512,1024]{1,0:T(8,128)}, bf16[512,1024]{1,0:T(8,128)(2,1)S(1)}, bf16[512,3072]{1,0:T(8,128)(2,1)}, f32[8,1024]{1,0:T(8,128)S(1)}) custom-call(s32[3]{0:T(128)S(1)} %copy-done.37, bf16[512,1024]{1,0:T(8,128)(2,1)S(1)} %copy-done.13, bf16[512,1024]{1,0:T(8,128)(2,1)S(1)} %copy-done.15, bf16[384,1024]{1,0:T(8,128)(2,1)S(1)} %copy-done.18, ...), custom_call_target="tpu_custom_call" | custom-call | flops 1073741824 | bytes 21041152 | tf_op jit(solution)/shard_map/pallas_call | solution.py:51
  257.3 5.8 %shard_map.197 = (f32[512,1024]{1,0:T(8,128)}, f32[8,1024]{1,0:T(8,128)S(1)}) custom-call(s32[3]{0:T(128)S(1)} %copy-done.37, bf16[512,1024]{1,0:T(8,128)(2,1)S(1)} %copy-done.12, f32[512,1024]{1,0:T(8,128)S(1)} %copy-done.8, f32[8,1024]{1,0:T(8,128)S(1)} %copy-done.34, f32[8,1024]{1,0:T(8,128)S(1)} %get-tuple-element.144.refs_4_, ...), custom_call_target="tpu_custom_call" | custom-call | flops 3221225472 | bytes 14778368 | tf_op jit(solution)/shard_map/pallas_call | solution.py:51
  265.2 6.7 %shard_map.198 = (bf16[512,512]{1,0:T(8,128)(2,1)S(1)}, bf16[512,512]{1,0:T(8,128)(2,1)S(1)}, bf16[512,512]{1,0:T(8,128)(2,1)S(1)}, bf16[512,512]{1,0:T(8,128)(2...) custom-call(s32[3]{0:T(128)S(1)} %copy-done.37, ...), custom_call_target="tpu_custom_call" | custom-call | flops 2147483648 | bytes 10485760 | tf_op jit(solution)/shard_map/pallas_call | solution.py:51
  275.3 6.6 %shard_map.199 = (bf16[512,512]{1,0:T(8,128)(2,1)S(1)}, bf16[512,512]{1,0:T(8,128)(2,1)S(1)}, bf16[512,512]{1,0:T(8,128)(2,1)S(1)}, bf16[512,512]{1,0:T(8,128)(2...) custom-call(s32[3]{0:T(128)S(1)} %copy-done.37, ...), custom_call_target="tpu_custom_call" | custom-call | flops 2147483648 | bytes 10485760 | tf_op jit(solution)/shard_map/pallas_call | solution.py:51
  289.2 12.1 %shard_map.201 = (bf16[512,1024]{1,0:T(8,128)(2,1)}, bf16[512,1024]{1,0:T(8,128)(2,1)}, bf16[512,1024]{1,0:T(8,128)(2,1)}, bf16[512,1024]{1,0:T(8,128)(2,1)}) custom-call(bf16[2048,1152]{1,0:T(8,128)(2,1)} %get-tuple-element.168.refs_4_.act_ref, bf16[1024,1152]{1,0:T(8,128)(2,1)} %all-gather.8.cloned.1.call-done.refs_5_.refs_6_.down_ref, ...), custom_call_target="tpu_custom_call" | custom-call | flops 4831838208 | bytes 11862016 | tf_op jit(solution)/shard_map/pallas_call | solution.py:421
  304.8 6.7 %collective-permute-done.49.refs_3_ = bf16[512,512]{1,0:T(8,128)(2,1)} collective-permute-done((bf16[512,512]{1,0:T(8,128)(2,1)}, bf16[512,512]{1,0:T(8,128)(2,1)}, u32[]{:S(2)}, u32[]{:S(2)}) %collective-permute-start.49) | collective-permute-done | bytes 524320 | tf_op jit(solution)/shard_map/ppermute | solution.py:635
  321.8 8.5 %collective-permute-done.45.refs_4_ = bf16[512,512]{1,0:T(8,128)(2,1)S(1)} collective-permute-done((bf16[512,512]{1,0:T(8,128)(2,1)S(1)}, bf16[512,512]{1,0:T(8,128)(2,1)S(1)}, u32[]{:S(2)}, u32[]{:S(2)}) %collective-permute-start.45) | collective-permute-done | bytes 524320 | tf_op jit(solution)/shard_map/ppermute | solution.py:635
  346.0 13.1 %collective-permute-done.53 = bf16[512,1024]{1,0:T(8,128)(2,1)} collective-permute-done((bf16[512,1024]{1,0:T(8,128)(2,1)S(1)}, bf16[512,1024]{1,0:T(8,128)(2,1)}, u32[]{:S(2)}, u32[]{:S(2)}) %collective-permute-start.53) | collective-permute-done | bytes 1048608 | tf_op jit(solution)/shard_map/ppermute | solution.py:638
  (298 shorter events, 124.6 us)
Async XLA Ops:
  7.2 70.7 %all-gather.4.cloned.1.call-start = ((), (), s32[]{:S(2)}) async-start(), calls=%async_computation.3 | async-start | bytes 1474560 | tf_op jit(solution)/shard_map/all_gather | solution.py:647
  15.8 24.9 %collective-permute-start.1 = (bf16[128,1152]{1,0:T(8,128)(2,1)S(1)}, bf16[128,1152]{1,0:T(8,128)(2,1)S(1)}, u32[]{:S(2)}, u32[]{:S(2)}) collective-permute-start(bf16[128,1152]{1,0:T(8,128)(2,1)S(1)} %shard_map.186.refs_1_), channel_id=1, source_target_pairs={{0,2},{1,3},{2,4},{3,5},{4,6},{5,7},{6,0},{7,1},{8,10},{9,11},{10,... | collective-permute-start | bytes 884744 | tf_op jit(solution)/shard_map/ppermute | solution.py:644
  41.4 62.8 %all-gather.6.cloned.1.call-start = ((), (), s32[]{:S(2)}) async-start(), calls=%async_computation.4 | async-start | bytes 1474560 | tf_op jit(solution)/shard_map/all_gather | solution.py:647
  42.8 111.1 %all-gather.8.cloned.1.call-start = ((), (), s32[]{:S(2)}) async-start(), calls=%async_computation.5 | async-start | bytes 2949120 | tf_op jit(solution)/shard_map/all_gather | solution.py:647
  77.9 26.4 %collective-permute-start.20 = (bf16[512,1152]{1,0:T(8,128)(2,1)}, bf16[512,1152]{1,0:T(8,128)(2,1)}, u32[]{:S(2)}, u32[]{:S(2)}) collective-permute-start(bf16[512,1152]{1,0:T(8,128)(2,1)} %all-gather.4.cloned.1.call-done.refs_4_), channel_id=1, source_target_pairs={{0,1},{1,0},{2,3},{3,2},{4,5},{5,4},{6,7},{7,6},{8,9},{9,8},{10,11... | collective-permute-start | bytes 3538952 | tf_op jit(solution)/shard_map/ppermute | solution.py:635
  78.2 26.1 %collective-permute-start.19 = (bf16[512,1024]{1,0:T(8,128)(2,1)S(1)}, bf16[512,1024]{1,0:T(8,128)(2,1)S(1)}, u32[]{:S(2)}, u32[]{:S(2)}) collective-permute-start(bf16[512,1024]{1,0:T(8,128)(2,1)S(1)} %copy-done.10), channel_id=1, source_target_pairs={{0,16},{8,24},{16,0},{24,8},{1,17},{9,25},{17,1},{25,9},{2,18},{10... | collective-permute-start | bytes 3145736 | tf_op jit(solution)/shard_map/ppermute | solution.py:638
  86.6 202.6 %reduce-scatter.4.cloned.1.call-start = ((), (), s32[]{:S(2)}) async-start(), calls=%async_computation.6 | async-start | bytes 2949120 | tf_op jit(solution)/shard_map/reduce_scatter | solution.py:650
  105.5 25.2 %collective-permute-start.24 = (bf16[512,1152]{1,0:T(8,128)(2,1)}, bf16[512,1152]{1,0:T(8,128)(2,1)S(1)}, u32[]{:S(2)}, u32[]{:S(2)}) collective-permute-start(bf16[512,1152]{1,0:T(8,128)(2,1)} %all-gather.6.cloned.1.call-done.refs_6_), channel_id=1, source_target_pairs={{0,1},{1,0},{2,3},{3,2},{4,5},{5,4},{6,7},{7,6},{8,9},{9,8},{10,11... | collective-permute-start | bytes 3538952 | tf_op jit(solution)/shard_map/ppermute | solution.py:635
  107.2 23.5 %collective-permute-start.21 = (bf16[512,1024]{1,0:T(8,128)(2,1)}, bf16[512,1024]{1,0:T(8,128)(2,1)S(1)}, u32[]{:S(2)}, u32[]{:S(2)}) collective-permute-start(bf16[512,1024]{1,0:T(8,128)(2,1)} %get-tuple-element.128.refs_0_), channel_id=1, source_target_pairs={{0,8},{8,0},{16,24},{24,16},{1,9},{9,1},{17,25},{25,17},{2,10},{10... | collective-permute-start | bytes 3145736 | tf_op jit(solution)/shard_map/ppermute | solution.py:641
  130.2 35.6 %collective-permute-start.26 = (bf16[512,1024]{1,0:T(8,128)(2,1)S(1)}, bf16[512,1024]{1,0:T(8,128)(2,1)}, u32[]{:S(2)}, u32[]{:S(2)}) collective-permute-start(bf16[512,1024]{1,0:T(8,128)(2,1)S(1)} %copy-done.10), channel_id=1, source_target_pairs={{0,8},{8,0},{16,24},{24,16},{1,9},{9,1},{17,25},{25,17},{2,10},{10... | collective-permute-start | bytes 3145736 | tf_op jit(solution)/shard_map/ppermute | solution.py:641
  176.9 28.8 %collective-permute-start.27 = (bf16[512,1152]{1,0:T(8,128)(2,1)}, bf16[512,1152]{1,0:T(8,128)(2,1)S(1)}, u32[]{:S(2)}, u32[]{:S(2)}) collective-permute-start(bf16[512,1152]{1,0:T(8,128)(2,1)} %get-tuple-element.125), channel_id=1, source_target_pairs={{0,1},{1,0},{2,3},{3,2},{4,5},{5,4},{6,7},{7,6},{8,9},{9,8},{10,11... | collective-permute-start | bytes 3538952 | tf_op jit(solution)/shard_map/ppermute | solution.py:635
  228.0 110.1 %reduce-scatter.8.cloned.1.call-start = ((), (), s32[]{:S(2)}) async-start(), calls=%async_computation.8 | async-start | bytes 1474560 | tf_op jit(solution)/shard_map/reduce_scatter | solution.py:650
  230.7 131.8 %reduce-scatter.6.cloned.1.call-start = ((), (), s32[]{:S(2)}) async-start(), calls=%async_computation.7 | async-start | bytes 1474560 | tf_op jit(solution)/shard_map/reduce_scatter | solution.py:650
  232.6 32.5 %collective-permute-start.30 = (bf16[256,1152]{1,0:T(8,128)(2,1)S(1)}, bf16[256,1152]{1,0:T(8,128)(2,1)S(1)}, u32[]{:S(2)}, u32[]{:S(2)}) collective-permute-start(bf16[256,1152]{1,0:T(8,128)(2,1)S(1)} %get-tuple-element.227), channel_id=1, source_target_pairs={{0,1},{1,0},{2,3},{3,2},{4,5},{5,4},{6,7},{7,6},{8,9},{9,8},{10,11... | collective-permute-start | bytes 1769480 | tf_op jit(solution)/shard_map/ppermute | solution.py:635
  232.9 41.8 %collective-permute-start.35 = (bf16[256,1152]{1,0:T(8,128)(2,1)S(1)}, bf16[256,1152]{1,0:T(8,128)(2,1)S(1)}, u32[]{:S(2)}, u32[]{:S(2)}) collective-permute-start(bf16[256,1152]{1,0:T(8,128)(2,1)S(1)} %get-tuple-element.226), channel_id=1, source_target_pairs={{0,1},{1,0},{2,3},{3,2},{4,5},{5,4},{6,7},{7,6},{8,9},{9,8},{10,11... | collective-permute-start | bytes 1769480 | tf_op jit(solution)/shard_map/ppermute | solution.py:635
  286.5 26.4 %collective-permute-start.42 = (bf16[512,512]{1,0:T(8,128)(2,1)}, bf16[512,512]{1,0:T(8,128)(2,1)S(1)}, u32[]{:S(2)}, u32[]{:S(2)}) collective-permute-start(bf16[512,512]{1,0:T(8,128)(2,1)} %get-tuple-element.167), channel_id=1, source_target_pairs={{0,16},{8,24},{16,0},{24,8},{1,17},{9,25},{17,1},{25,9},{2,18},{10... | collective-permute-start | bytes 1572872 | tf_op jit(solution)/shard_map/ppermute | solution.py:638
  286.9 26.0 %collective-permute-start.47 = (bf16[512,512]{1,0:T(8,128)(2,1)}, bf16[512,512]{1,0:T(8,128)(2,1)S(1)}, u32[]{:S(2)}, u32[]{:S(2)}) collective-permute-start(bf16[512,512]{1,0:T(8,128)(2,1)} %get-tuple-element.179), channel_id=1, source_target_pairs={{0,1},{1,0},{2,3},{3,2},{4,5},{5,4},{6,7},{7,6},{8,9},{9,8},{10,11... | collective-permute-start | bytes 1572872 | tf_op jit(solution)/shard_map/ppermute | solution.py:635
  287.9 23.6 %collective-permute-start.49 = (bf16[512,512]{1,0:T(8,128)(2,1)}, bf16[512,512]{1,0:T(8,128)(2,1)}, u32[]{:S(2)}, u32[]{:S(2)}) collective-permute-start(bf16[512,512]{1,0:T(8,128)(2,1)} %get-tuple-element.182), channel_id=1, source_target_pairs={{0,1},{1,0},{2,3},{3,2},{4,5},{5,4},{6,7},{7,6},{8,9},{9,8},{10,11... | collective-permute-start | bytes 1572872 | tf_op jit(solution)/shard_map/ppermute | solution.py:635
  301.3 33.2 %collective-permute-start.52 = (bf16[512,1024]{1,0:T(8,128)(2,1)}, bf16[512,1024]{1,0:T(8,128)(2,1)}, u32[]{:S(2)}, u32[]{:S(2)}) collective-permute-start(bf16[512,1024]{1,0:T(8,128)(2,1)} %get-tuple-element.186), channel_id=1, source_target_pairs={{0,8},{8,0},{16,24},{24,16},{1,9},{9,1},{17,25},{25,17},{2,10},{10... | collective-permute-start | bytes 3145736 | tf_op jit(solution)/shard_map/ppermute | solution.py:641
  318.9 27.1 %collective-permute-start.40 = (bf16[512,1024]{1,0:T(8,128)(2,1)}, bf16[512,1024]{1,0:T(8,128)(2,1)}, u32[]{:S(2)}, u32[]{:S(2)}) collective-permute-start(bf16[512,1024]{1,0:T(8,128)(2,1)} %get-tuple-element.171), channel_id=1, source_target_pairs={{0,8},{8,0},{16,24},{24,16},{1,9},{9,1},{17,25},{25,17},{2,10},{10... | collective-permute-start | bytes 3145736 | tf_op jit(solution)/shard_map/ppermute | solution.py:641
  336.2 22.9 %collective-permute-start.53 = (bf16[512,1024]{1,0:T(8,128)(2,1)S(1)}, bf16[512,1024]{1,0:T(8,128)(2,1)}, u32[]{:S(2)}, u32[]{:S(2)}) collective-permute-start(bf16[512,1024]{1,0:T(8,128)(2,1)S(1)} %shard_map.206), channel_id=1, source_target_pairs={{0,16},{8,24},{16,0},{24,8},{1,17},{9,25},{17,1},{25,9},{2,18},{10... | collective-permute-start | bytes 3145736 | tf_op jit(solution)/shard_map/ppermute | solution.py:638
  339.3 24.2 %collective-permute-start.54 = (bf16[128,1152]{1,0:T(8,128)(2,1)}, bf16[128,1152]{1,0:T(8,128)(2,1)}, u32[]{:S(2)}, u32[]{:S(2)}) collective-permute-start(bf16[128,1152]{1,0:T(8,128)(2,1)} %get-tuple-element.187), channel_id=1, source_target_pairs={{0,2},{1,3},{2,4},{3,5},{4,6},{5,7},{6,0},{7,1},{8,10},{9,11},{10,... | collective-permute-start | bytes 884744 | tf_op jit(solution)/shard_map/ppermute | solution.py:644
  341.5 23.7 %collective-permute-start.55 = (bf16[128,1152]{1,0:T(8,128)(2,1)}, bf16[128,1152]{1,0:T(8,128)(2,1)}, u32[]{:S(2)}, u32[]{:S(2)}) collective-permute-start(bf16[128,1152]{1,0:T(8,128)(2,1)} %get-tuple-element.188), channel_id=1, source_target_pairs={{0,4},{1,5},{2,6},{3,7},{4,0},{5,1},{6,2},{7,3},{8,12},{9,13},{10,... | collective-permute-start | bytes 884744 | tf_op jit(solution)/shard_map/ppermute | solution.py:644
  344.4 24.1 %collective-permute-start.56 = (bf16[128,1152]{1,0:T(8,128)(2,1)}, bf16[128,1152]{1,0:T(8,128)(2,1)}, u32[]{:S(2)}, u32[]{:S(2)}) collective-permute-start(bf16[128,1152]{1,0:T(8,128)(2,1)} %get-tuple-element.189), channel_id=1, source_target_pairs={{0,6},{1,7},{2,0},{3,1},{4,2},{5,3},{6,4},{7,5},{8,14},{9,15},{10,... | collective-permute-start | bytes 884744 | tf_op jit(solution)/shard_map/ppermute | solution.py:644
  (110 other events, 1324.7 us)
Sparse Core Ops, SparseCore 0:
  41.5 30.4 all-gather.3
  73.6 29.5 all-gather.5
  105.3 48.4 all-gather.7
  228.1 45.3 reduce-scatter.3
  275.6 29.0 reduce-scatter.7
  314.9 27.7 reduce-scatter.5

commit v2 on v1

--- a/solution.py
+++ b/solution.py
@@ -385,11 +385,11 @@
 TILE = 256
 
 
-def piece_specs(pieces, count, width):
-    tiles = count // TILE
+def piece_specs(pieces, count, width, tile=TILE):
+    tiles = count // tile
     return [
         pl.BlockSpec(
-            (TILE, width), lambda t, k=k: (jnp.clip(t - k * tiles, 0, tiles - 1), 0)
+            (tile, width), lambda t, k=k: (jnp.clip(t - k * tiles, 0, tiles - 1), 0)
         )
         for k in range(pieces)
     ]
@@ -455,13 +455,14 @@
 def act_call(rows, scalars, pieces, woven):
     count, width = pieces[0].shape
     inner = woven[0].shape[1]
-    tiles = count // TILE
-    wide = pl.BlockSpec((TILE, inner), lambda t: (t, 0))
+    tile = count
+    tiles = count // tile
+    wide = pl.BlockSpec((tile, inner), lambda t: (t, 0))
     weight = shape((width, inner), LINK)
     return tiled(
         functools.partial(act_kernel, tiles, rows),
         4 * tiles,
-        [SCALARS] + piece_specs(4, count, width) + [whole_spec(v) for v in woven],
+        [SCALARS] + piece_specs(4, count, width, tile) + [whole_spec(v) for v in woven],
         [scalars, *pieces, *woven],
         [wide] * 3 + [whole_spec(weight)] * 2,
         [shape((4 * count, inner), LINK)] * 3 + [weight] * 2,

time: 383 us -> 383 us (level)
  no operation moved by 1% of the time
where the time goes in v2:
time: 383 us; the launch traced here: 379 us
  Pallas kernels  155 us (40%)
  waiting for transfers between devices  98.5 us (26%)
  starting transfers between devices  73.2 us (19%)
  local copies, waits for them, and re-layouts  28 us (7%)
  between operations  15 us (4%)
  other arithmetic  9.94 us (3%)
    pallas_call x7, Pallas kernels, tiled(): pl.pallas_call(kernel, grid=(grid,), in_specs=in_specs, out_specs=out_spe...  94.3 us
    pallas_call x15, Pallas kernels, call(): pl.pallas_call(run, out_shape=outs, in_specs=[SCALARS] + [WHOLE] * len(ar...  60.2 us
    ppermute x25, starting transfers between devices, swap_core(): return lax.ppermute(v, 'dp', [(i, i ^ 1) for i in range(columns)])  41.4 us
    ppermute x15, waiting for transfers between devices, swap_row(): return lax.ppermute(v, 'fsdp', [(i, i ^ 1) for i in range(ways)])  35.2 us
    ppermute x12, waiting for transfers between devices, swap_far(): return lax.ppermute(v, 'dp', [(i, i ^ 2) for i in range(columns)])  33.3 us
    unnamed x142, local copies, waits for them, and re-layouts  24.1 us
    ppermute x6, waiting for transfers between devices, shift_high(): lax.ppermute(v, 'fsdp', [(i, (i + 2 * s) % ways) for i in range(ways)])  23.6 us
    ppermute x15, starting transfers between devices, swap_row(): return lax.ppermute(v, 'fsdp', [(i, i ^ 1) for i in range(ways)])  12.1 us
  transfers between devices with their start and end apart: 64, of which 20 were waited for; matrix products, arithmetic and copies ran while one was open for 4% of the time, Pallas kernels for 35%

profile of v2, /device:TPU:9, one launch (start us, length us, event | category | flops | bytes accessed | tf_op | source)
XLA Modules:
  0.0 379.2 jit_solution(2970055341600516946)
XLA Ops:
  22.2 12.2 %collective-permute-done.2.refs_3_ = bf16[128,1152]{1,0:T(8,128)(2,1)S(1)} collective-permute-done((bf16[128,1152]{1,0:T(8,128)(2,1)S(1)}, bf16[128,1152]{1,0:T(8,128)(2,1)S(1)}, u32[]{:S(2)}, u32[]{:S(2)}) %collective-permute-start.2) | collective-permute-done | bytes 294944 | tf_op jit(solution)/shard_map/ppermute | solution.py:645
  34.4 6.3 %collective-permute-done.1.refs_2_ = bf16[128,1152]{1,0:T(8,128)(2,1)S(1)} collective-permute-done((bf16[128,1152]{1,0:T(8,128)(2,1)S(1)}, bf16[128,1152]{1,0:T(8,128)(2,1)S(1)}, u32[]{:S(2)}, u32[]{:S(2)}) %collective-permute-start.1) | collective-permute-done | bytes 294944 | tf_op jit(solution)/shard_map/ppermute | solution.py:645
  46.7 10.9 %collective-permute-done.4.refs_4_ = bf16[512,128]{1,0:T(8,128)(2,1)S(1)} collective-permute-done((bf16[512,128]{1,0:T(8,128)(2,1)S(1)}, bf16[512,128]{1,0:T(8,128)(2,1)S(1)}, u32[]{:S(2)}, u32[]{:S(2)}) %collective-permute-start.4) | collective-permute-done | bytes 131104 | tf_op jit(solution)/shard_map/ppermute | solution.py:636
  58.5 4.2 %collective-permute-start.6 = (bf16[512,512]{1,0:T(8,128)(2,1)S(1)}, bf16[512,512]{1,0:T(8,128)(2,1)S(1)}, u32[]{:S(2)}, u32[]{:S(2)}) collective-permute-start(bf16[512,512]{1,0:T(8,128)(2,1)S(1)} %get-tuple-element.108.refs_5_), channel_id=1, source_target_pairs={{0,8},{8,0},{16,24},{24,16},{1,9},{9,1},{17,25},{25,17},{2,10},{10... | collective-permute-start | bytes 1572872 | tf_op jit(solution)/shard_map/ppermute | solution.py:642
  64.2 4.6 %collective-permute-done.12.refs_14_ = bf16[512,512]{1,0:T(8,128)(2,1)} collective-permute-done((bf16[512,512]{1,0:T(8,128)(2,1)S(1)}, bf16[512,512]{1,0:T(8,128)(2,1)}, u32[]{:S(2)}, u32[]{:S(2)}) %collective-permute-start.12) | collective-permute-done | bytes 524320 | tf_op jit(solution)/shard_map/ppermute | solution.py:636
  69.1 8.0 %collective-permute-start.14 = (bf16[512,512]{1,0:T(8,128)(2,1)}, bf16[512,512]{1,0:T(8,128)(2,1)}, u32[]{:S(2)}, u32[]{:S(2)}) collective-permute-start(bf16[512,512]{1,0:T(8,128)(2,1)} %collective-permute-done.12.refs_14_), channel_id=1, source_target_pairs={{0,8},{8,0},{16,24},{24,16},{1,9},{9,1},{17,25},{25,17},{2,10},{10... | collective-permute-start | bytes 1572872 | tf_op jit(solution)/shard_map/ppermute | solution.py:642
  80.1 5.7 %collective-permute-start.7 = (bf16[512,512]{1,0:T(8,128)(2,1)}, bf16[512,512]{1,0:T(8,128)(2,1)}, u32[]{:S(2)}, u32[]{:S(2)}) collective-permute-start(bf16[512,512]{1,0:T(8,128)(2,1)} %copy-done.64), channel_id=1, source_target_pairs={{0,8},{8,0},{16,24},{24,16},{1,9},{9,1},{17,25},{25,17},{2,10},{10... | collective-permute-start | bytes 1572872 | tf_op jit(solution)/shard_map/ppermute | solution.py:642
  89.3 15.0 %shard_map.188 = (bf16[512,1024]{1,0:T(8,128)(2,1)}, f32[3,512,1024]{2,1,0:T(8,128)}, bf16[512,1024]{1,0:T(8,128)(2,1)}, f32[512,1024]{1,0:T(8,128)}, bf16[512,1...) custom-call(s32[3]{0:T(128)} %copy-done.35, ...), custom_call_target="tpu_custom_call" | custom-call | flops 4294967296 | bytes 29659136 | tf_op jit(solution)/shard_map/pallas_call | solution.py:51
  110.5 14.4 %collective-permute-done.22.refs_2_ = bf16[512,1024]{1,0:T(8,128)(2,1)S(1)} collective-permute-done((bf16[512,1024]{1,0:T(8,128)(2,1)}, bf16[512,1024]{1,0:T(8,128)(2,1)S(1)}, u32[]{:S(2)}, u32[]{:S(2)}) %collective-permute-start.22) | collective-permute-done | bytes 1048608 | tf_op jit(solution)/shard_map/ppermute | solution.py:639
  124.9 5.3 %collective-permute-start.23 = (bf16[512,1024]{1,0:T(8,128)(2,1)S(1)}, bf16[512,1024]{1,0:T(8,128)(2,1)S(1)}, u32[]{:S(2)}, u32[]{:S(2)}) collective-permute-start(bf16[512,1024]{1,0:T(8,128)(2,1)S(1)} %collective-permute-done.22.refs_2_), channel_id=1, source_target_pairs={{0,8},{8,0},{16,24},{24,16},{1,9},{9,1},{17,25},{25,17},{2,10},{10... | collective-permute-start | bytes 3145736 | tf_op jit(solution)/shard_map/ppermute | solution.py:642
  133.4 18.2 %shard_map.189 = (bf16[2048,1152]{1,0:T(8,128)(2,1)}, bf16[2048,1152]{1,0:T(8,128)(2,1)}, bf16[2048,1152]{1,0:T(8,128)(2,1)}, bf16[1024,1152]{1,0:T(8,128)(2,1)}, bf16[1024,1152]{1,0:T(8,128)(2,1)}) custom-call(s32[3]{0:T(128)} %copy-done.35, bf16[512,1024]{1,0:T(8,128)(2,1)} %get-tuple-element.128.refs_0_, bf16[512,1024]{1,0:T(8,128)(2,1)} %copy-done.62, ...), custom_call_target="tpu_custom_call" | custom-call | flops 9663676416 | bytes 27787276 | tf_op jit(solution)/shard_map/pallas_call | solution.py:421
  153.9 9.6 %shard_map.190 = (bf16[512,1152]{1,0:T(8,128)(2,1)}, bf16[512,1152]{1,0:T(8,128)(2,1)}, bf16[512,1024]{1,0:T(8,128)(2,1)}) custom-call(bf16[512,1024]{1,0:T(8,128)(2,1)} %copy-done.52, bf16[2048,1152]{1,0:T(8,128)(2,1)} %get-tuple-element.117.refs_1_.refs_2_, bf16[2048,1152]{1,0:T(8,128)(2,1)} %get-tuple-element.118.refs_2_.refs_3_, ...), custom_call_target="tpu_custom_call" | custom-call | flops 3623878656 | bytes 20971520 | tf_op jit(solution)/shard_map/pallas_call | solution.py:421
  165.5 11.2 %shard_map.191 = (f32[512,1152]{1,0:T(8,128)}, bf16[512,1152]{1,0:T(8,128)(2,1)}) custom-call(s32[3]{0:T(128)} %copy-done.35, bf16[512,1024]{1,0:T(8,128)(2,1)} %refs_6_.1, bf16[512,1024]{1,0:T(8,128)(2,1)} %collective-permute-done.26.refs_1_, bf16[512,1024]{1,0:T(8,128)(2,1)} %copy-done.51, bf16[512,1024]{1,0:T(8,128)(2,1)} %copy-done.52, ...), custom_call_target="tpu_custom_call" | custom-call | flops 4831838208 | bytes 12451852 | tf_op jit(solution)/shard_map/pallas_call | solution.py:421
  179.1 10.0 %shard_map.193 = (bf16[512,1152]{1,0:T(8,128)(2,1)}, bf16[512,1152]{1,0:T(8,128)(2,1)}, bf16[512,1024]{1,0:T(8,128)(2,1)}) custom-call(bf16[512,1024]{1,0:T(8,128)(2,1)} %copy-done.51, bf16[2048,1152]{1,0:T(8,128)(2,1)} %get-tuple-element.117.refs_1_.refs_2_, bf16[2048,1152]{1,0:T(8,128)(2,1)} %get-tuple-element.118.refs_2_.refs_3_, ...), custom_call_target="tpu_custom_call" | custom-call | flops 3623878656 | bytes 22020096 | tf_op jit(solution)/shard_map/pallas_call | solution.py:421
  190.7 14.7 %shard_map.194 = (bf16[1024,1152]{1,0:T(8,128)(2,1)}, bf16[1024,1152]{1,0:T(8,128)(2,1)}, bf16[512,1024]{1,0:T(8,128)(2,1)}, bf16[512,1024]{1,0:T(8,128)(2,1)}) custom-call(bf16[512,1024]{1,0:T(8,128)(2,1)} %refs_6_.1, bf16[512,1024]{1,0:T(8,128)(2,1)} %collective-permute-done.26.refs_1_, bf16[2048,1152]{1,0:T(8,128)(2,1)} %get-tuple-element.117.refs_1_.refs_2_, ...), custom_call_target="tpu_custom_call" | custom-call | flops 7247757312 | bytes 25427968 | tf_op jit(solution)/shard_map/pallas_call | solution.py:421
  209.2 18.5 %shard_map.195 = (f32[512,1152]{1,0:T(8,128)}, bf16[512,1152]{1,0:T(8,128)(2,1)}, bf16[1024,1152]{1,0:T(8,128)(2,1)}) custom-call(s32[3]{0:T(128)} %copy-done.35, bf16[512,1024]{1,0:T(8,128)(2,1)} %get-tuple-element.128.refs_0_, bf16[512,1024]{1,0:T(8,128)(2,1)} %copy-done.62, bf16[512,1024]{1,0:T(8,128)(2,1)} %copy-done.61, bf16[512,1024]{1,0:T(8,128)(2,1)} %copy-done.63, ...), custom_call_target="tpu_custom_call" | custom-call | flops 9663676416 | bytes 19529740 | tf_op jit(solution)/shard_map/pallas_call | solution.py:421
  242.6 11.0 %shard_map.196 = (f32[512,1024]{1,0:T(8,128)}, bf16[512,1024]{1,0:T(8,128)(2,1)S(1)}, bf16[512,3072]{1,0:T(8,128)(2,1)}, f32[8,1024]{1,0:T(8,128)S(1)}) custom-call(s32[3]{0:T(128)S(1)} %copy-done.37, bf16[512,1024]{1,0:T(8,128)(2,1)S(1)} %copy-done.13, bf16[512,1024]{1,0:T(8,128)(2,1)S(1)} %copy-done.15, bf16[384,1024]{1,0:T(8,128)(2,1)S(1)} %copy-done.18, ...), custom_call_target="tpu_custom_call" | custom-call | flops 1073741824 | bytes 21041152 | tf_op jit(solution)/shard_map/pallas_call | solution.py:51
  257.1 5.8 %shard_map.197 = (f32[512,1024]{1,0:T(8,128)}, f32[8,1024]{1,0:T(8,128)S(1)}) custom-call(s32[3]{0:T(128)S(1)} %copy-done.37, bf16[512,1024]{1,0:T(8,128)(2,1)S(1)} %copy-done.12, f32[512,1024]{1,0:T(8,128)S(1)} %copy-done.8, f32[8,1024]{1,0:T(8,128)S(1)} %copy-done.34, f32[8,1024]{1,0:T(8,128)S(1)} %get-tuple-element.144.refs_4_, ...), custom_call_target="tpu_custom_call" | custom-call | flops 3221225472 | bytes 14778368 | tf_op jit(solution)/shard_map/pallas_call | solution.py:51
  265.0 6.7 %shard_map.198 = (bf16[512,512]{1,0:T(8,128)(2,1)S(1)}, bf16[512,512]{1,0:T(8,128)(2,1)S(1)}, bf16[512,512]{1,0:T(8,128)(2,1)S(1)}, bf16[512,512]{1,0:T(8,128)(2...) custom-call(s32[3]{0:T(128)S(1)} %copy-done.37, ...), custom_call_target="tpu_custom_call" | custom-call | flops 2147483648 | bytes 10485760 | tf_op jit(solution)/shard_map/pallas_call | solution.py:51
  275.0 6.6 %shard_map.199 = (bf16[512,512]{1,0:T(8,128)(2,1)S(1)}, bf16[512,512]{1,0:T(8,128)(2,1)S(1)}, bf16[512,512]{1,0:T(8,128)(2,1)S(1)}, bf16[512,512]{1,0:T(8,128)(2...) custom-call(s32[3]{0:T(128)S(1)} %copy-done.37, ...), custom_call_target="tpu_custom_call" | custom-call | flops 2147483648 | bytes 10485760 | tf_op jit(solution)/shard_map/pallas_call | solution.py:51
  288.9 12.1 %shard_map.201 = (bf16[512,1024]{1,0:T(8,128)(2,1)}, bf16[512,1024]{1,0:T(8,128)(2,1)}, bf16[512,1024]{1,0:T(8,128)(2,1)}, bf16[512,1024]{1,0:T(8,128)(2,1)}) custom-call(bf16[2048,1152]{1,0:T(8,128)(2,1)} %get-tuple-element.168.refs_4_.act_ref, bf16[1024,1152]{1,0:T(8,128)(2,1)} %all-gather.8.cloned.1.call-done.refs_5_.refs_6_.down_ref, ...), custom_call_target="tpu_custom_call" | custom-call | flops 4831838208 | bytes 11862016 | tf_op jit(solution)/shard_map/pallas_call | solution.py:421
  304.5 6.7 %collective-permute-done.49.refs_3_ = bf16[512,512]{1,0:T(8,128)(2,1)} collective-permute-done((bf16[512,512]{1,0:T(8,128)(2,1)}, bf16[512,512]{1,0:T(8,128)(2,1)}, u32[]{:S(2)}, u32[]{:S(2)}) %collective-permute-start.49) | collective-permute-done | bytes 524320 | tf_op jit(solution)/shard_map/ppermute | solution.py:636
  321.5 8.5 %collective-permute-done.45.refs_4_ = bf16[512,512]{1,0:T(8,128)(2,1)S(1)} collective-permute-done((bf16[512,512]{1,0:T(8,128)(2,1)S(1)}, bf16[512,512]{1,0:T(8,128)(2,1)S(1)}, u32[]{:S(2)}, u32[]{:S(2)}) %collective-permute-start.45) | collective-permute-done | bytes 524320 | tf_op jit(solution)/shard_map/ppermute | solution.py:636
  346.0 12.9 %collective-permute-done.53 = bf16[512,1024]{1,0:T(8,128)(2,1)} collective-permute-done((bf16[512,1024]{1,0:T(8,128)(2,1)S(1)}, bf16[512,1024]{1,0:T(8,128)(2,1)}, u32[]{:S(2)}, u32[]{:S(2)}) %collective-permute-start.53) | collective-permute-done | bytes 1048608 | tf_op jit(solution)/shard_map/ppermute | solution.py:639
  (298 shorter events, 124.8 us)
Async XLA Ops:
  7.2 70.7 %all-gather.4.cloned.1.call-start = ((), (), s32[]{:S(2)}) async-start(), calls=%async_computation.3 | async-start | bytes 1474560 | tf_op jit(solution)/shard_map/all_gather | solution.py:648
  15.8 24.9 %collective-permute-start.1 = (bf16[128,1152]{1,0:T(8,128)(2,1)S(1)}, bf16[128,1152]{1,0:T(8,128)(2,1)S(1)}, u32[]{:S(2)}, u32[]{:S(2)}) collective-permute-start(bf16[128,1152]{1,0:T(8,128)(2,1)S(1)} %shard_map.186.refs_1_), channel_id=1, source_target_pairs={{0,2},{1,3},{2,4},{3,5},{4,6},{5,7},{6,0},{7,1},{8,10},{9,11},{10,... | collective-permute-start | bytes 884744 | tf_op jit(solution)/shard_map/ppermute | solution.py:645
  41.4 62.8 %all-gather.6.cloned.1.call-start = ((), (), s32[]{:S(2)}) async-start(), calls=%async_computation.4 | async-start | bytes 1474560 | tf_op jit(solution)/shard_map/all_gather | solution.py:648
  42.8 111.1 %all-gather.8.cloned.1.call-start = ((), (), s32[]{:S(2)}) async-start(), calls=%async_computation.5 | async-start | bytes 2949120 | tf_op jit(solution)/shard_map/all_gather | solution.py:648
  77.9 26.4 %collective-permute-start.20 = (bf16[512,1152]{1,0:T(8,128)(2,1)}, bf16[512,1152]{1,0:T(8,128)(2,1)}, u32[]{:S(2)}, u32[]{:S(2)}) collective-permute-start(bf16[512,1152]{1,0:T(8,128)(2,1)} %all-gather.4.cloned.1.call-done.refs_4_), channel_id=1, source_target_pairs={{0,1},{1,0},{2,3},{3,2},{4,5},{5,4},{6,7},{7,6},{8,9},{9,8},{10,11... | collective-permute-start | bytes 3538952 | tf_op jit(solution)/shard_map/ppermute | solution.py:636
  78.2 26.1 %collective-permute-start.19 = (bf16[512,1024]{1,0:T(8,128)(2,1)S(1)}, bf16[512,1024]{1,0:T(8,128)(2,1)S(1)}, u32[]{:S(2)}, u32[]{:S(2)}) collective-permute-start(bf16[512,1024]{1,0:T(8,128)(2,1)S(1)} %copy-done.10), channel_id=1, source_target_pairs={{0,16},{8,24},{16,0},{24,8},{1,17},{9,25},{17,1},{25,9},{2,18},{10... | collective-permute-start | bytes 3145736 | tf_op jit(solution)/shard_map/ppermute | solution.py:639
  86.6 202.3 %reduce-scatter.4.cloned.1.call-start = ((), (), s32[]{:S(2)}) async-start(), calls=%async_computation.6 | async-start | bytes 2949120 | tf_op jit(solution)/shard_map/reduce_scatter | solution.py:651
  105.5 25.2 %collective-permute-start.24 = (bf16[512,1152]{1,0:T(8,128)(2,1)}, bf16[512,1152]{1,0:T(8,128)(2,1)S(1)}, u32[]{:S(2)}, u32[]{:S(2)}) collective-permute-start(bf16[512,1152]{1,0:T(8,128)(2,1)} %all-gather.6.cloned.1.call-done.refs_6_), channel_id=1, source_target_pairs={{0,1},{1,0},{2,3},{3,2},{4,5},{5,4},{6,7},{7,6},{8,9},{9,8},{10,11... | collective-permute-start | bytes 3538952 | tf_op jit(solution)/shard_map/ppermute | solution.py:636
  107.2 23.5 %collective-permute-start.21 = (bf16[512,1024]{1,0:T(8,128)(2,1)}, bf16[512,1024]{1,0:T(8,128)(2,1)S(1)}, u32[]{:S(2)}, u32[]{:S(2)}) collective-permute-start(bf16[512,1024]{1,0:T(8,128)(2,1)} %get-tuple-element.128.refs_0_), channel_id=1, source_target_pairs={{0,8},{8,0},{16,24},{24,16},{1,9},{9,1},{17,25},{25,17},{2,10},{10... | collective-permute-start | bytes 3145736 | tf_op jit(solution)/shard_map/ppermute | solution.py:642
  130.2 35.3 %collective-permute-start.26 = (bf16[512,1024]{1,0:T(8,128)(2,1)S(1)}, bf16[512,1024]{1,0:T(8,128)(2,1)}, u32[]{:S(2)}, u32[]{:S(2)}) collective-permute-start(bf16[512,1024]{1,0:T(8,128)(2,1)S(1)} %copy-done.10), channel_id=1, source_target_pairs={{0,8},{8,0},{16,24},{24,16},{1,9},{9,1},{17,25},{25,17},{2,10},{10... | collective-permute-start | bytes 3145736 | tf_op jit(solution)/shard_map/ppermute | solution.py:642
  176.7 28.8 %collective-permute-start.27 = (bf16[512,1152]{1,0:T(8,128)(2,1)}, bf16[512,1152]{1,0:T(8,128)(2,1)S(1)}, u32[]{:S(2)}, u32[]{:S(2)}) collective-permute-start(bf16[512,1152]{1,0:T(8,128)(2,1)} %get-tuple-element.125), channel_id=1, source_target_pairs={{0,1},{1,0},{2,3},{3,2},{4,5},{5,4},{6,7},{7,6},{8,9},{9,8},{10,11... | collective-permute-start | bytes 3538952 | tf_op jit(solution)/shard_map/ppermute | solution.py:636
  227.7 110.1 %reduce-scatter.8.cloned.1.call-start = ((), (), s32[]{:S(2)}) async-start(), calls=%async_computation.8 | async-start | bytes 1474560 | tf_op jit(solution)/shard_map/reduce_scatter | solution.py:651
  230.4 131.8 %reduce-scatter.6.cloned.1.call-start = ((), (), s32[]{:S(2)}) async-start(), calls=%async_computation.7 | async-start | bytes 1474560 | tf_op jit(solution)/shard_map/reduce_scatter | solution.py:651
  232.4 32.5 %collective-permute-start.30 = (bf16[256,1152]{1,0:T(8,128)(2,1)S(1)}, bf16[256,1152]{1,0:T(8,128)(2,1)S(1)}, u32[]{:S(2)}, u32[]{:S(2)}) collective-permute-start(bf16[256,1152]{1,0:T(8,128)(2,1)S(1)} %get-tuple-element.227), channel_id=1, source_target_pairs={{0,1},{1,0},{2,3},{3,2},{4,5},{5,4},{6,7},{7,6},{8,9},{9,8},{10,11... | collective-permute-start | bytes 1769480 | tf_op jit(solution)/shard_map/ppermute | solution.py:636
  232.6 41.9 %collective-permute-start.35 = (bf16[256,1152]{1,0:T(8,128)(2,1)S(1)}, bf16[256,1152]{1,0:T(8,128)(2,1)S(1)}, u32[]{:S(2)}, u32[]{:S(2)}) collective-permute-start(bf16[256,1152]{1,0:T(8,128)(2,1)S(1)} %get-tuple-element.226), channel_id=1, source_target_pairs={{0,1},{1,0},{2,3},{3,2},{4,5},{5,4},{6,7},{7,6},{8,9},{9,8},{10,11... | collective-permute-start | bytes 1769480 | tf_op jit(solution)/shard_map/ppermute | solution.py:636
  286.2 26.4 %collective-permute-start.42 = (bf16[512,512]{1,0:T(8,128)(2,1)}, bf16[512,512]{1,0:T(8,128)(2,1)S(1)}, u32[]{:S(2)}, u32[]{:S(2)}) collective-permute-start(bf16[512,512]{1,0:T(8,128)(2,1)} %get-tuple-element.167), channel_id=1, source_target_pairs={{0,16},{8,24},{16,0},{24,8},{1,17},{9,25},{17,1},{25,9},{2,18},{10... | collective-permute-start | bytes 1572872 | tf_op jit(solution)/shard_map/ppermute | solution.py:639
  286.6 26.0 %collective-permute-start.47 = (bf16[512,512]{1,0:T(8,128)(2,1)}, bf16[512,512]{1,0:T(8,128)(2,1)S(1)}, u32[]{:S(2)}, u32[]{:S(2)}) collective-permute-start(bf16[512,512]{1,0:T(8,128)(2,1)} %get-tuple-element.179), channel_id=1, source_target_pairs={{0,1},{1,0},{2,3},{3,2},{4,5},{5,4},{6,7},{7,6},{8,9},{9,8},{10,11... | collective-permute-start | bytes 1572872 | tf_op jit(solution)/shard_map/ppermute | solution.py:636
  287.6 23.6 %collective-permute-start.49 = (bf16[512,512]{1,0:T(8,128)(2,1)}, bf16[512,512]{1,0:T(8,128)(2,1)}, u32[]{:S(2)}, u32[]{:S(2)}) collective-permute-start(bf16[512,512]{1,0:T(8,128)(2,1)} %get-tuple-element.182), channel_id=1, source_target_pairs={{0,1},{1,0},{2,3},{3,2},{4,5},{5,4},{6,7},{7,6},{8,9},{9,8},{10,11... | collective-permute-start | bytes 1572872 | tf_op jit(solution)/shard_map/ppermute | solution.py:636
  301.0 33.2 %collective-permute-start.52 = (bf16[512,1024]{1,0:T(8,128)(2,1)}, bf16[512,1024]{1,0:T(8,128)(2,1)}, u32[]{:S(2)}, u32[]{:S(2)}) collective-permute-start(bf16[512,1024]{1,0:T(8,128)(2,1)} %get-tuple-element.186), channel_id=1, source_target_pairs={{0,8},{8,0},{16,24},{24,16},{1,9},{9,1},{17,25},{25,17},{2,10},{10... | collective-permute-start | bytes 3145736 | tf_op jit(solution)/shard_map/ppermute | solution.py:642
  318.7 27.4 %collective-permute-start.40 = (bf16[512,1024]{1,0:T(8,128)(2,1)}, bf16[512,1024]{1,0:T(8,128)(2,1)}, u32[]{:S(2)}, u32[]{:S(2)}) collective-permute-start(bf16[512,1024]{1,0:T(8,128)(2,1)} %get-tuple-element.171), channel_id=1, source_target_pairs={{0,8},{8,0},{16,24},{24,16},{1,9},{9,1},{17,25},{25,17},{2,10},{10... | collective-permute-start | bytes 3145736 | tf_op jit(solution)/shard_map/ppermute | solution.py:642
  336.0 23.0 %collective-permute-start.53 = (bf16[512,1024]{1,0:T(8,128)(2,1)S(1)}, bf16[512,1024]{1,0:T(8,128)(2,1)}, u32[]{:S(2)}, u32[]{:S(2)}) collective-permute-start(bf16[512,1024]{1,0:T(8,128)(2,1)S(1)} %shard_map.206), channel_id=1, source_target_pairs={{0,16},{8,24},{16,0},{24,8},{1,17},{9,25},{17,1},{25,9},{2,18},{10... | collective-permute-start | bytes 3145736 | tf_op jit(solution)/shard_map/ppermute | solution.py:639
  339.0 24.3 %collective-permute-start.54 = (bf16[128,1152]{1,0:T(8,128)(2,1)}, bf16[128,1152]{1,0:T(8,128)(2,1)}, u32[]{:S(2)}, u32[]{:S(2)}) collective-permute-start(bf16[128,1152]{1,0:T(8,128)(2,1)} %get-tuple-element.187), channel_id=1, source_target_pairs={{0,2},{1,3},{2,4},{3,5},{4,6},{5,7},{6,0},{7,1},{8,10},{9,11},{10,... | collective-permute-start | bytes 884744 | tf_op jit(solution)/shard_map/ppermute | solution.py:645
  341.3 23.7 %collective-permute-start.55 = (bf16[128,1152]{1,0:T(8,128)(2,1)}, bf16[128,1152]{1,0:T(8,128)(2,1)}, u32[]{:S(2)}, u32[]{:S(2)}) collective-permute-start(bf16[128,1152]{1,0:T(8,128)(2,1)} %get-tuple-element.188), channel_id=1, source_target_pairs={{0,4},{1,5},{2,6},{3,7},{4,0},{5,1},{6,2},{7,3},{8,12},{9,13},{10,... | collective-permute-start | bytes 884744 | tf_op jit(solution)/shard_map/ppermute | solution.py:645
  344.1 24.2 %collective-permute-start.56 = (bf16[128,1152]{1,0:T(8,128)(2,1)}, bf16[128,1152]{1,0:T(8,128)(2,1)}, u32[]{:S(2)}, u32[]{:S(2)}) collective-permute-start(bf16[128,1152]{1,0:T(8,128)(2,1)} %get-tuple-element.189), channel_id=1, source_target_pairs={{0,6},{1,7},{2,0},{3,1},{4,2},{5,3},{6,4},{7,5},{8,14},{9,15},{10,... | collective-permute-start | bytes 884744 | tf_op jit(solution)/shard_map/ppermute | solution.py:645
  (110 other events, 1324.3 us)
Sparse Core Ops, SparseCore 0:
  41.5 30.4 all-gather.3
  73.6 29.5 all-gather.5
  105.3 48.4 all-gather.7
  227.8 45.3 reduce-scatter.3
  275.3 29.0 reduce-scatter.7
  314.6 27.7 reduce-scatter.5
